TPU v7x, 256 devices: a whole 4x4x8 slice. The times are simulated.
256 devices in a mesh: dp: 8 (over y, z_lo), frame: 32 (over z_hi, x, core).
Axes of the slice: x: 4, y: 4, z: 8 (z_hi: 4, z_lo: 2; z = z_hi * 2 + z_lo), core: 2. Of those that a mesh axis runs over, the one named last changes fastest.
Arguments:
- recorded_exposures: float32 [16, 128, 128, 128], P('dp', 'frame'), may hold values from -6 to 6
- aberration_phase_screens: float32 [44, 16384], replicated, may hold values from -0.875 to 0.875
- entry_convolution_kernel: float32 [256, 256], replicated, may hold values from -0.375 to 0.375
- residual_inner_map: float32 [256, 256], replicated, may hold values from -0.375 to 0.375
- residual_outer_map: float32 [256, 256], replicated, may hold values from -0.375 to 0.375
- output_projection_kernel: float32 [256, 44], replicated, may hold values from -0.375 to 0.375
Outputs:
- phase_weights_derivative: float32 [16, 128, 44], P('dp', 'frame')
- grad_embed: float32 [256, 256], replicated
- grad_first: float32 [256, 256], replicated
- grad_second: float32 [256, 256], replicated
- grad_head: float32 [256, 44], replicated
- patch_loss: float32 [16], P('dp')
All inputs are finite; a program needn't handle non-finite values.
Results may differ from a plain program's by a relative error of at most 0.0003.
Values sent between devices are 32-bit elements; how exact they have to be, the bound alone decides.
A program may use at most 64 MiB of HBM per device.

v0:
```python
import functools
import types

import jax
import jax.numpy as jnp
import numpy as np
from jax import lax
from jax.experimental import pallas as pl
from jax.experimental.pallas import tpu as pltpu
from jax.sharding import PartitionSpec as P

entry_block_length = 16
regularizer_relative = 0.001
MESH = pl.DeviceIdType.MESH
HIGH = lax.Precision.HIGH
HIGHEST = lax.Precision.HIGHEST
side = 128
half = side // 2
span = half + 1
pad_span = 72
images = 8
frames_here = 4
modes = 44
tiles_each = 64
loss_lane = 64


def dot(a, b, precision=HIGH):
    return jnp.dot(a, b, precision=precision, preferred_element_type=jnp.float32)


def dot_tn(a, b, precision=HIGH):
    return lax.dot_general(
        a, b, (((0,), (0,)), ((), ())), precision=precision, preferred_element_type=jnp.float32
    )


def dot_nt(a, b, precision=HIGH):
    return lax.dot_general(
        a, b, (((1,), (1,)), ((), ())), precision=precision, preferred_element_type=jnp.float32
    )


def transform_tables():
    index = np.arange(side)
    angle = 2.0 * np.pi / side * (index[:, None] * index[None, :] % side)
    c, s = np.cos(angle), np.sin(angle)
    both = np.block([[c, -s], [s, c]])
    lo = slice(0, half)
    half_plane = np.concatenate([both[:, lo], both[:, side : side + half]], axis=1)
    swapped = np.concatenate([half_plane, half_plane[:, half:], half_plane[:, :half]], axis=1)
    rows = slice(half // 2, half // 2 + span)
    pupil = np.zeros((2 * side, 2 * pad_span))
    pupil[:side, :span], pupil[:side, pad_span : pad_span + span] = c[:, rows], s[:, rows]
    pupil[side:, :span], pupil[side:, pad_span : pad_span + span] = -s[:, rows], c[:, rows]
    real = np.concatenate([c, -s], axis=0)
    tables = (both, both.T, pupil, pupil.T, real, real.T, half_plane, half_plane.T, swapped / side)
    return tuple(np.ascontiguousarray(t.astype(np.float32)) for t in tables)


def aperture_area():
    at = np.arange(side) - half
    return float(np.sum(at[:, None] ** 2 + at[None, :] ** 2 <= (side // 4) ** 2))


def sigmoid(value):
    return 1.0 / (1.0 + jnp.exp(-value))


def silu_act(value):
    return value / (1.0 + jnp.exp(-value))


def silu_slope(value):
    gate = sigmoid(value)
    return gate * (1.0 + value * (1.0 - gate))


def alternating(rows):
    lane = lax.broadcasted_iota(jnp.int32, (rows, side), 1)
    return jnp.where(lax.rem(lane, 2) == 0, 1.0, -1.0).astype(jnp.float32)


def corner(rows):
    row = lax.broadcasted_iota(jnp.int32, (rows, side), 0)
    lane = lax.broadcasted_iota(jnp.int32, (rows, side), 1)
    return jnp.logical_and(row == 0, lax.rem(lane, half) == 0)


def cut_tiles(img, tiles):
    group = lax.broadcasted_iota(jnp.int32, (8, side), 1) // 16

    def one(n, carry):
        for g in range(2):
            x = [img[n, pl.ds(8 * g + j, 8, stride=16), :] for j in range(8)]
            for bit in (1, 2, 4):
                low = lax.rem(group // bit, 2) == 0
                y = list(x)
                for p in range(8):
                    if p & bit == 0:
                        q = p + bit
                        y[p] = jnp.where(low, x[p], pltpu.roll(x[q], 16 * bit, 1))
                        y[q] = jnp.where(low, pltpu.roll(x[p], side - 16 * bit, 1), x[q])
                x = y
            for c in range(8):
                tiles[pl.ds(pl.multiple_of(n * 64 + c * 8, 8), 8), g * side : (g + 1) * side] = x[c]
        return carry

    lax.fori_loop(0, images, one, 0)


def tile_sum(value):
    return jnp.sum(value.reshape(images, tiles_each, value.shape[1]), axis=1)


def encode(tiles, embed, first, second, head, hid_pre, inn_pre, inner_sum, pooled):
    pre = dot(tiles[...], embed[...], HIGHEST)
    hid_pre[...] = pre
    hidden = silu_act(pre)
    pre2 = dot(hidden, first[...], HIGHEST)
    inn_pre[...] = pre2
    total = tile_sum(silu_act(pre2))
    inner_sum[...] = total
    mean = (tile_sum(hidden) + dot(total, second[...], HIGHEST)) * (1.0 / tiles_each)
    pooled[...] = mean
    return dot(mean, head[...], HIGHEST)


def pupil_field(alpha, screens, spread, field):
    for m in range(modes):
        spread[m] = jnp.broadcast_to(alpha[:, m : m + 1], (images, side))
    lane = lax.broadcasted_iota(jnp.int32, (images, side), 1) - half
    width = 5

    def rows(block, carry):
        at = [pl.multiple_of((block * width + i) * side, side) for i in range(width)]
        total = [jnp.zeros((images, side), jnp.float32) for _ in range(width)]
        for m in range(modes):
            weight = spread[m]
            for i in range(width):
                total[i] = total[i] + weight * screens[m : m + 1, pl.ds(at[i], side)]
        for i in range(width):
            up = block * width + i - half // 2
            inside = lane * lane + up * up <= (side // 4) ** 2
            field[block * width + i, :, 0:side] = jnp.where(inside, jnp.cos(total[i]), 0.0)
            field[block * width + i, :, side : 2 * side] = jnp.where(inside, jnp.sin(total[i]), 0.0)
        return carry

    lax.fori_loop(0, span // width, rows, 0)
    for i in range(span, pad_span):
        field[i] = jnp.zeros((images, 2 * side), jnp.float32)


def real_transform(planes, real, table, staged, out, alt):
    staged[...] = dot(real[...], planes)
    edge = []
    for n in range(images):
        lanes = slice(n * side, (n + 1) * side)
        edge.append(jnp.sum(staged[0:1, lanes] * alt, axis=1, keepdims=True))
        pair = jnp.concatenate([staged[0:side, lanes], staged[side : 2 * side, lanes]], axis=1)
        out[n] = dot(pair, table[...])
    return edge


def forward(img, screens, embed, first, second, head, tables, s):
    both, _, pupil, _, real, _, half_plane, _, swapped = tables
    alt = alternating(1)
    slot = jnp.logical_and(
        lax.broadcasted_iota(jnp.int32, (8, 2 * side), 0) == 0,
        lax.broadcasted_iota(jnp.int32, (8, 2 * side), 1) == half,
    )
    cut_tiles(img, s.tiles)
    alpha = encode(s.tiles, embed, first, second, head, s.hid_pre, s.inn_pre, s.inner_sum, s.pooled)
    planes = jnp.concatenate([img[n] for n in range(images)], axis=1)
    edge = real_transform(planes, real, swapped, s.staged, s.spec, alt)
    for n in range(images):
        s.spec[n, 0:8, :] = jnp.where(slot, edge[n] * (1.0 / side), s.spec[n, 0:8, :])
        s.energy[n : n + 1, :] = jnp.sum(img[n] * img[n], axis=0, keepdims=True)
    s.wait_screens()
    pupil_field(alpha, screens, s.spread, s.field)
    rowed = dot(s.field[...].reshape(pad_span * images, 2 * side), both[...])
    s.rowed_r[...] = rowed[:, 0:side]
    s.rowed_i[...] = rowed[:, side : 2 * side]
    for n in range(images):
        lanes = slice(n * side, (n + 1) * side)
        rows = pl.ds(n, pad_span, stride=images)
        s.stack[0:pad_span, lanes] = s.rowed_r[rows, :]
        s.stack[pad_span : 2 * pad_span, lanes] = s.rowed_i[rows, :]
    s.focal[...] = dot(pupil[...], s.stack[...])
    scale = 1.0 / (side * side * aperture_area())
    fr, fi = s.focal[0:side, :], s.focal[side : 2 * side, :]
    spot = (fr * fr + fi * fi) * scale
    edge = real_transform(spot, real, half_plane, s.staged, s.otf, alt)
    lane = lax.broadcasted_iota(jnp.int32, (side, side), 1)
    real_slot, at_corner = lane < half, corner(side)
    for n in range(images):
        s.otf[n, 0:8, :] = jnp.where(slot[:, :side], edge[n], s.otf[n, 0:8, :])
    for p in range(images // frames_here):
        t1 = t2 = t3 = None
        for f in range(frames_here):
            n = p * frames_here + f
            o, a, b = s.otf[n], s.spec[n, :, 0:side], s.spec[n, :, side : 2 * side]
            t1 = a * o if t1 is None else t1 + a * o
            t2 = b * o if t2 is None else t2 + b * o
            t3 = o * o if t3 is None else t3 + o * o
        turned = pltpu.roll(t2, half, 1)
        num = jnp.where(real_slot, t1 + pltpu.roll(t1, half, 1), turned - t2)
        num = jnp.where(at_corner, t1, num)
        den = jnp.where(at_corner, t3, t3 + pltpu.roll(t3, half, 1))
        s.part[p * 16 : (p + 1) * 16, 0:8, :] = num.reshape(16, 8, side)
        s.part[p * 16 : (p + 1) * 16, 8:16, :] = den.reshape(16, 8, side)


def backward(screens, tables, s):
    _, both_t, _, pupil_t, _, real_t, _, half_plane_t, _ = tables
    lane = lax.broadcasted_iota(jnp.int32, (side, side), 1)
    real_slot, at_corner = lane < half, corner(side)
    alt = alternating(1)
    per_pixel = 1.0 / (side * side)
    weight = jnp.where(lax.rem(lane, half) == 0, per_pixel, 2.0 * per_pixel)
    losses = []
    for p in range(images // frames_here):
        rho = s.ratio[p * 16 : (p + 1) * 16].reshape(side, side)
        num = s.part[p * 16 : (p + 1) * 16, 0:8, :].reshape(side, side)
        turned = pltpu.roll(rho, half, 1)
        square = rho * rho
        a = jnp.where(jnp.logical_or(real_slot, at_corner), rho, turned) * (-2.0 * weight)
        b = jnp.where(real_slot, turned, -rho)
        b = jnp.where(at_corner, 0.0, b) * (-2.0 * weight)
        m = jnp.where(at_corner, square, square + turned * turned) * (2.0 * weight)
        explained = jnp.sum(jnp.sum(weight * rho * num, axis=0, keepdims=True), axis=1, keepdims=True)
        energy = s.energy[p * frames_here : (p + 1) * frames_here, :]
        energy = jnp.sum(jnp.sum(energy, axis=0, keepdims=True), axis=1, keepdims=True)
        losses.append(energy * per_pixel - explained)
        for f in range(frames_here):
            n = p * frames_here + f
            lanes = slice(n * side, (n + 1) * side)
            g = a * s.spec[n, :, 0:side] + b * s.spec[n, :, side : 2 * side] + m * s.otf[n]
            y = dot(g, half_plane_t[...])
            s.staged[0:side, lanes] = y[:, 0:side]
            s.staged[side : 2 * side, lanes] = y[:, side : 2 * side]
            s.staged[0:1, lanes] = y[0:1, 0:side] + g[0:1, half : half + 1] * alt
    d_spot = dot(real_t[...], s.staged[...]) * (2.0 / (side * side * aperture_area()))
    d_focal = jnp.concatenate([s.focal[0:side, :] * d_spot, s.focal[side : 2 * side, :] * d_spot], axis=0)
    s.stack[...] = dot(pupil_t[...], d_focal)
    for n in range(images):
        lanes = slice(n * side, (n + 1) * side)
        rows = pl.ds(n, pad_span, stride=images)
        s.rowed_r[rows, :] = s.stack[0:pad_span, lanes]
        s.rowed_i[rows, :] = s.stack[pad_span : 2 * pad_span, lanes]
    rowed = jnp.concatenate([s.rowed_r[...], s.rowed_i[...]], axis=1)
    d_field = dot(rowed, both_t[...]).reshape(pad_span, images, 2 * side)
    f_r, f_i = s.field[:, :, 0:side], s.field[:, :, side : 2 * side]
    s.phase[...] = d_field[:, :, side : 2 * side] * f_r - d_field[:, :, 0:side] * f_i

    alpha_lane = lax.broadcasted_iota(jnp.int32, (images, side), 1)
    d_alpha = jnp.zeros((images, side), jnp.float32)
    chunk = 11
    for start in range(0, modes, chunk):

        def rows(i, total, start=start):
            value = s.phase[i]
            at = pl.multiple_of(i * side, side)
            return tuple(
                total[m] + value * screens[start + m : start + m + 1, pl.ds(at, side)]
                for m in range(chunk)
            )

        zero = tuple(jnp.zeros((images, side), jnp.float32) for _ in range(chunk))
        total = lax.fori_loop(0, span, rows, zero)
        for m in range(chunk):
            d_alpha = jnp.where(
                alpha_lane == start + m, jnp.sum(total[m], axis=1, keepdims=True), d_alpha
            )
    return d_alpha, losses


def encoder_gradients(d_alpha, tiles, embed, first, second, head, s):
    d_alpha44 = d_alpha[:, 0:modes]
    d_pooled = dot_nt(d_alpha44, head[...]) * (1.0 / tiles_each)
    s.grad_head[:, 0:side] = dot_tn(s.pooled[...], d_alpha)
    s.grad_second[...] = dot_tn(s.inner_sum[...], d_pooled)
    d_inner = dot_nt(d_pooled, second[...])
    width = embed.shape[1]

    def spread(value):
        return jnp.broadcast_to(value[:, None, :], (images, tiles_each, width)).reshape(-1, width)

    d_inner_pre = spread(d_inner) * silu_slope(s.inn_pre[...])
    s.grad_first[...] = dot_tn(silu_act(s.hid_pre[...]), d_inner_pre)
    d_hidden = spread(d_pooled) + dot_nt(d_inner_pre, first[...])
    s.grad_embed[...] = dot_tn(tiles[...], d_hidden * silu_slope(s.hid_pre[...]))


state_shapes = dict(
    tiles=(images * tiles_each, 256),
    hid_pre=(images * tiles_each, 256),
    inn_pre=(images * tiles_each, 256),
    inner_sum=(images, 256),
    pooled=(images, 256),
    energy=(images, side),
    spread=(modes, images, side),
    field=(pad_span, images, 2 * side),
    rowed_r=(pad_span * images, side),
    rowed_i=(pad_span * images, side),
    stack=(2 * pad_span, images * side),
    focal=(2 * side, images * side),
    staged=(2 * side, images * side),
    spec=(images, side, 2 * side),
    otf=(images, side, side),
    part=(32, 16, side),
    inbox=(32, 16, side),
    ratio=(32, 8, side),
    phase=(pad_span, images, side),
    screens=(modes, span * side),
)
gradient_shapes = dict(
    grad_embed=(256, 256), grad_first=(256, 256), grad_second=(256, 256), grad_head=(256, side), grad_tail=(128, 256)
)


class Place:
    def __init__(self):
        self.dp, self.frame = lax.axis_index("dp"), lax.axis_index("frame")
        self.core, self.x = lax.rem(self.frame, 2), lax.rem(self.frame // 2, 4)
        self.y, self.z_lo = self.dp // 2, lax.rem(self.dp, 2)
        self.z = (self.frame // 8) * 2 + self.z_lo

    def device(self, core, x, y, z):
        return {"dp": y * 2 + lax.rem(z, 2), "frame": (z // 2) * 8 + x * 2 + core}

    def x_peer(self, step):
        return lax.rem(self.x + step, 4)

    def y_peer(self, step):
        return lax.rem(self.y + step, 4)

    def z_peer(self, step):
        return lax.rem(self.z + step, 8)


def greet(group):
    place = Place()
    barrier = pltpu.get_barrier_semaphore()

    def one(step, carry):
        target = {"frame": lax.rem(place.frame + step, group)}
        pl.semaphore_signal(barrier, inc=1, device_id=target, device_id_type=MESH)
        return carry

    lax.fori_loop(1, group, one, 0)
    others = [place.device(place.core, place.x, place.y_peer(s), place.z) for s in range(1, 4)]
    others += [place.device(place.core, place.x, place.y, place.z_peer(s)) for s in (1, 3, 5, 7)]
    for target in others:
        pl.semaphore_signal(barrier, inc=1, device_id=target, device_id_type=MESH)
    return group - 1 + len(others)


def spectral_exchange(s, group, sems):
    me = lax.axis_index("frame")

    def peer(step):
        return lax.rem(me + step, group)

    def scatter_copy(step):
        return pltpu.make_async_remote_copy(
            src_ref=s.part.at[peer(step)],
            dst_ref=s.inbox.at[step],
            send_sem=sems.at[0, step],
            recv_sem=sems.at[1, step],
            device_id={"frame": peer(step)},
            device_id_type=MESH,
        )

    def gather_copy(step):
        return pltpu.make_async_remote_copy(
            src_ref=s.ratio.at[me],
            dst_ref=s.ratio.at[me],
            send_sem=sems.at[2, step],
            recv_sem=sems.at[3, step],
            device_id={"frame": peer(step)},
            device_id_type=MESH,
        )

    def start(copy):
        def one(step, carry):
            copy(step).start()
            return carry

        lax.fori_loop(1, group, one, 0)

    start(scatter_copy)

    def add(step, total):
        scatter_copy(step).wait_recv()
        return total + s.inbox[step]

    total = lax.fori_loop(1, group, add, s.part[me])
    s.ratio[me] = total[0:8] / (total[8:16] + regularizer_relative * (group * frames_here))
    start(gather_copy)

    def finish(step, carry):
        scatter_copy(step).wait_send()
        gather_copy(step).wait()
        return carry

    lax.fori_loop(1, group, finish, 0)


part_rows = (256, 256, 256, 128)


def buffer_shapes(half_width):
    shapes = [(r, half_width) for r in part_rows]
    shapes += [(r, half_width) for r in part_rows]
    shapes += [(3, r // 4, half_width) for r in part_rows]
    shapes += [(r // 4, half_width) for r in part_rows]
    shapes += [(3, r // 16, half_width) for r in part_rows]
    shapes += [(8, 8, half_width), (7, 8, half_width), (8, 8, half_width)]
    shapes += [(4, 8, 8, half_width), (4, 4, 8, 8, half_width), (4, 4, 8, 8, half_width)]
    return shapes


def gradient_exchange(parts, out_ref, buffers, sems):
    core_in, sums, x_in, x_sums, y_in = (buffers[4 * i : 4 * i + 4] for i in range(5))
    zone, z_in, z_all, y_all, x_all, core_all = buffers[20:]
    place = Place()
    core, x, y, z = place.core, place.x, place.y, place.z
    device, x_peer, y_peer, z_peer = place.device, place.x_peer, place.y_peer, place.z_peer
    core_peer = device(1 - core, x, y, z)

    used = [0]

    def copy(src, dst, target):
        slot = used[0]
        used[0] += 1
        one = pltpu.make_async_remote_copy(
            src_ref=src,
            dst_ref=dst,
            send_sem=sems.at[0, slot],
            recv_sem=sems.at[1, slot],
            device_id=target,
            device_id_type=MESH,
        )
        one.start()
        return one

    sent = []
    lanes = parts[0].shape[1] // 2
    mine = pl.ds(pl.multiple_of(core * lanes, lanes), lanes)
    other = pl.ds(pl.multiple_of((1 - core) * lanes, lanes), lanes)
    core_copies = [copy(parts[p].at[:, other], core_in[p], core_peer) for p in range(4)]
    sent += core_copies

    x_copies = []
    for p in range(4):
        core_copies[p].wait_recv()
        sums[p][...] = parts[p][:, mine] + core_in[p][...]
        size = part_rows[p] // 4
        x_copies.append([
            copy(
                sums[p].at[pl.ds(pl.multiple_of(x_peer(s) * size, size), size)],
                x_in[p].at[s - 1],
                device(core, x_peer(s), y, z),
            )
            for s in range(1, 4)
        ])
        sent += x_copies[p]

    y_copies = []
    for p in range(4):
        for one in x_copies[p]:
            one.wait_recv()
        size = part_rows[p] // 4
        own = sums[p][pl.ds(pl.multiple_of(x * size, size), size)]
        x_sums[p][...] = own + x_in[p][0] + x_in[p][1] + x_in[p][2]
        size = part_rows[p] // 16
        y_copies.append([
            copy(
                x_sums[p].at[pl.ds(pl.multiple_of(y_peer(s) * size, size), size)],
                y_in[p].at[s - 1],
                device(core, x, y_peer(s), z),
            )
            for s in range(1, 4)
        ])
        sent += y_copies[p]

    at = 0
    for p in range(4):
        for one in y_copies[p]:
            one.wait_recv()
        size = part_rows[p] // 16
        own = x_sums[p][pl.ds(pl.multiple_of(y * size, size), size)]
        total = own + y_in[p][0] + y_in[p][1] + y_in[p][2]
        for row in range(0, size, 8):
            zone[at // 8] = total[row : row + 8]
            at += 8
    zone[7] = jnp.zeros_like(zone[7])

    z_copies = [
        copy(zone.at[z_peer(s)], z_in.at[s - 1], device(core, x, y, z_peer(s))) for s in range(1, 8)
    ]
    sent += z_copies
    total = zone[z]
    for s in range(1, 8):
        z_copies[s - 1].wait_recv()
        total = total + z_in[s - 1]
    z_all[z] = total
    z_gather = [
        copy(z_all.at[z], z_all.at[z], device(core, x, y, z_peer(s))) for s in range(1, 8)
    ]
    sent += z_gather
    for one in z_gather:
        one.wait_recv()

    y_all[y] = z_all[...]
    y_gather = [
        copy(y_all.at[y], y_all.at[y], device(core, x, y_peer(s), z)) for s in range(1, 4)
    ]
    sent += y_gather
    for one in y_gather:
        one.wait_recv()

    x_all[x] = y_all[...]
    x_gather = [
        copy(x_all.at[x], x_all.at[x], device(core, x_peer(s), y, z)) for s in range(1, 4)
    ]
    sent += x_gather
    core_gather = [copy(x_all.at[x], core_all.at[x], core_peer)]
    for s in range(1, 4):
        x_gather[s - 1].wait_recv()
        came_from = lax.rem(x + 4 - s, 4)
        core_gather.append(copy(x_all.at[came_from], core_all.at[came_from], core_peer))
    sent += core_gather
    for one in core_gather:
        one.wait_recv()

    starts = (0, 2, 4, 6)
    for p in range(4):
        quarter, size = part_rows[p] // 4, part_rows[p] // 16
        base = p * 256
        for px in range(4):
            for py in range(4):
                for row in range(0, size, 8):
                    at = base + px * quarter + py * size + row
                    tile = starts[p] + row // 8
                    out_ref[at : at + 8, mine] = x_all[px, py, tile]
                    out_ref[at : at + 8, other] = core_all[px, py, tile]
    for one in sent:
        one.wait_send()


def kernel(names, group, *refs):
    img, screens_hbm, embed, first, second, head = refs[:6]
    tables, (alpha_ref, total_ref), scratch = refs[6:15], refs[15:17], refs[17:]
    s = types.SimpleNamespace(**dict(zip(names, scratch)))
    buffers = scratch[len(names) : -3]
    screens_sem, spectral_sems, gradient_sems = scratch[-3:]
    greeted = greet(group)
    fetch = pltpu.make_async_copy(
        screens_hbm.at[:, pl.ds(half // 2 * side, span * side)], s.screens, screens_sem
    )
    fetch.start()
    s.wait_screens = fetch.wait
    forward(img, s.screens, embed, first, second, head, tables, s)
    pl.semaphore_wait(pltpu.get_barrier_semaphore(), greeted)
    spectral_exchange(s, group, spectral_sems)
    d_alpha, losses = backward(s.screens, tables, s)
    alpha_ref[...] = d_alpha
    encoder_gradients(d_alpha, s.tiles, embed, first, second, head, s)
    s.grad_tail[:, 0:side] = s.grad_head[0:side, :]
    s.grad_tail[:, side : 2 * side] = s.grad_head[side : 2 * side, :]
    lane = lax.broadcasted_iota(jnp.int32, (1, side), 1)
    top = s.grad_tail[0:1, 0:side]
    for p in range(len(losses)):
        at = loss_lane + lax.axis_index("dp") * len(losses) + p
        top = jnp.where(lane == at, losses[p], top)
    s.grad_tail[0:1, 0:side] = top
    parts = (s.grad_embed, s.grad_first, s.grad_second, s.grad_tail)
    gradient_exchange(parts, total_ref, buffers, gradient_sems)


def local(recorded_exposures, screens, embed, first, second, head):
    regions = recorded_exposures.shape[0]
    group = lax.axis_size("frame")
    f32 = jnp.float32
    names = list(state_shapes) + list(gradient_shapes)
    shapes = list(state_shapes.values()) + list(gradient_shapes.values()) + buffer_shapes(side)
    vmem = pl.BlockSpec(memory_space=pltpu.VMEM)
    d_alpha, total = pl.pallas_call(
        functools.partial(kernel, names, group),
        out_shape=[
            jax.ShapeDtypeStruct((images, side), f32),
            jax.ShapeDtypeStruct((sum(part_rows), 2 * side), f32),
        ],
        in_specs=[vmem, pl.BlockSpec(memory_space=pl.ANY)] + [vmem] * 13,
        out_specs=[vmem] * 2,
        scratch_shapes=[pltpu.VMEM(shape, f32) for shape in shapes]
        + [
            pltpu.SemaphoreType.DMA(()),
            pltpu.SemaphoreType.DMA((4, group)),
            pltpu.SemaphoreType.DMA((2, 64)),
        ],
        compiler_params=pltpu.CompilerParams(
            collective_id=0, has_side_effects=True, vmem_limit_bytes=48 << 20
        ),
    )(
        recorded_exposures.reshape(images, side, side),
        screens, embed, first, second, head, *transform_tables(),
    )
    tail = total[768:]
    start = loss_lane + lax.axis_index("dp") * regions
    losses = lax.dynamic_slice(tail, (0, start), (1, regions))[0]
    return (
        d_alpha[:, :modes].reshape(regions, -1, modes),
        total[:256],
        total[256:512],
        total[512:768],
        jnp.concatenate([tail[:, :modes], tail[:, side : side + modes]], axis=0),
        losses / (group * frames_here),
    )


def solution(mesh):
    return jax.shard_map(
        local,
        mesh=mesh,
        in_specs=(P("dp", "frame", None, None), P(), P(), P(), P(), P()),
        out_specs=(P("dp", "frame", None), P(), P(), P(), P(), P("dp")),
        check_vma=False,
    )
```

profile of v0, /device:TPU:1, one launch (start us, length us, event | category | flops | bytes accessed | tf_op | source)
XLA Modules:
  0.0 90.9 jit_solution(18072659353842955009)
XLA Ops:
  0.6 0.9 copy.23.refs_5_
  1.5 0.0 copy-start
  1.5 1.0 %copy-done = f32[2,4,128,128]{3,2,1,0:T(8,128)S(1)} copy-done((f32[2,4,128,128]{3,2,1,0:T(8,128)S(1)}, f32[2,4,128,128]{3,2,1,0:T(8,128)}, u32[]{:S(2)}) %copy-start) | copy-done | bytes 524312
  2.6 0.9 %copy-done.1 = f32[256,256]{1,0:T(8,128)S(1)} copy-done((f32[256,256]{1,0:T(8,128)S(1)}, f32[256,256]{1,0:T(8,128)}, u32[]{:S(2)}) %copy-start.1) | copy-done | bytes 262168
  3.5 0.0 copy-start.2
  3.5 0.9 %copy-done.2 = f32[256,256]{1,0:T(8,128)S(1)} copy-done((f32[256,256]{1,0:T(8,128)S(1)}, f32[256,256]{1,0:T(8,128)}, u32[]{:S(2)}) %copy-start.2) | copy-done | bytes 262168
  4.5 0.0 copy-start.3
  4.5 0.9 %copy-done.3 = f32[256,256]{1,0:T(8,128)S(1)} copy-done((f32[256,256]{1,0:T(8,128)S(1)}, f32[256,256]{1,0:T(8,128)}, u32[]{:S(2)}) %copy-start.3) | copy-done | bytes 262168
  5.4 0.0 copy-start.4
  5.4 0.9 %copy-done.4 = f32[256,256]{1,0:T(8,128)S(1)} copy-done((f32[256,256]{1,0:T(8,128)S(1)}, f32[256,256]{1,0:T(8,128)}, u32[]{:S(2)}) %copy-start.4) | copy-done | bytes 262168
  6.4 0.0 copy-start.5
  6.4 0.9 %copy-done.5 = f32[256,256]{1,0:T(8,128)S(1)} copy-done((f32[256,256]{1,0:T(8,128)S(1)}, f32[256,256]{1,0:T(8,128)}, u32[]{:S(2)}) %copy-start.5) | copy-done | bytes 262168
  7.3 0.0 copy-start.6
  7.3 0.9 %copy-done.6 = f32[256,144]{1,0:T(8,128)S(1)} copy-done((f32[256,144]{1,0:T(8,128)S(1)}, f32[256,144]{1,0:T(8,128)}, u32[]{:S(2)}) %copy-start.6) | copy-done | bytes 147480
  8.3 0.0 copy-start.7
  8.3 0.9 %copy-done.7 = f32[256,256]{1,0:T(8,128)S(1)} copy-done((f32[256,256]{1,0:T(8,128)S(1)}, f32[256,256]{1,0:T(8,128)}, u32[]{:S(2)}) %copy-start.7) | copy-done | bytes 262168
  9.2 0.0 copy-start.8
  9.2 0.9 copy-done.8
  10.1 0.0 copy-start.9
  10.1 0.9 copy-done.9
  11.0 0.0 copy-start.10
  11.0 0.9 copy-done.10
  11.9 0.0 copy-start.11
  12.0 0.9 copy-done.11
  12.9 0.9 copy-done.12
  13.8 74.2 %shard_map.190 = (f32[8,128]{1,0:T(8,128)S(1)}, f32[896,256]{1,0:T(8,128)S(1)}) custom-call(f32[8,128,128]{2,1,0:T(8,128)S(1)} %bitcast.5, f32[44,16384]{1,0:T(8,128)} %refs_1_.1, f32[256,256]{1,0:T(8,128)S(1)} %copy-done.1, f32[256,256]{1,0:T(8,128)S(1)} %copy-done.2, f32[256,256]{1,0:T(8,128)S(1)} %copy-done.3, f32[256,44]{1,0:T(8,128)S(1)} %copy.23.refs_5_, ...), custom_call_target="tpu_custom_call" | custom-call | tf_op jit(solution)/shard_map/pallas_call | solution.py:590
  88.0 0.1 copy.24
  88.1 0.1 copy.25
  88.2 0.7 pad_maximum_fusion
  88.8 0.6 multiply_bitcast_fusion
  89.4 0.9 fusion.1
  90.3 0.6 copy.27
  (4 shorter events, 0.0 us)
Async XLA Ops:
  1.5 1.0 %copy-start = (f32[2,4,128,128]{3,2,1,0:T(8,128)S(1)}, f32[2,4,128,128]{3,2,1,0:T(8,128)}, u32[]{:S(2)}) copy-start(f32[2,4,128,128]{3,2,1,0:T(8,128)} %param.15) | copy-start | bytes 1572868
  2.6 0.9 %copy-start.1 = (f32[256,256]{1,0:T(8,128)S(1)}, f32[256,256]{1,0:T(8,128)}, u32[]{:S(2)}) copy-start(f32[256,256]{1,0:T(8,128)} %refs_2_.1) | copy-start | bytes 786436
  3.5 0.9 %copy-start.2 = (f32[256,256]{1,0:T(8,128)S(1)}, f32[256,256]{1,0:T(8,128)}, u32[]{:S(2)}) copy-start(f32[256,256]{1,0:T(8,128)} %refs_3_.1) | copy-start | bytes 786436
  4.5 0.9 %copy-start.3 = (f32[256,256]{1,0:T(8,128)S(1)}, f32[256,256]{1,0:T(8,128)}, u32[]{:S(2)}) copy-start(f32[256,256]{1,0:T(8,128)} %refs_4_.1) | copy-start | bytes 786436
  5.4 0.9 %copy-start.4 = (f32[256,256]{1,0:T(8,128)S(1)}, f32[256,256]{1,0:T(8,128)}, u32[]{:S(2)}) copy-start(f32[256,256]{1,0:T(8,128)} %constant.36.clone.refs_6_) | copy-start | bytes 786436
  6.4 0.9 %copy-start.5 = (f32[256,256]{1,0:T(8,128)S(1)}, f32[256,256]{1,0:T(8,128)}, u32[]{:S(2)}) copy-start(f32[256,256]{1,0:T(8,128)} %constant.37.clone.refs_7_) | copy-start | bytes 786436
  7.3 0.9 %copy-start.6 = (f32[256,144]{1,0:T(8,128)S(1)}, f32[256,144]{1,0:T(8,128)}, u32[]{:S(2)}) copy-start(f32[256,144]{1,0:T(8,128)} %constant.38.clone.refs_8_) | copy-start | bytes 442372
  8.3 0.9 %copy-start.7 = (f32[256,256]{1,0:T(8,128)S(1)}, f32[256,256]{1,0:T(8,128)}, u32[]{:S(2)}) copy-start(f32[256,256]{1,0:T(8,128)} %constant.44.clone.refs_14_) | copy-start | bytes 786436
  9.2 0.9 %copy-start.8 = (f32[144,256]{1,0:T(8,128)S(1)}, f32[144,256]{1,0:T(8,128)}, u32[]{:S(2)}) copy-start(f32[144,256]{1,0:T(8,128)} %constant.39.clone.refs_9_) | copy-start | bytes 442372
  10.1 0.9 copy-start.9
  11.0 0.9 copy-start.10
  11.9 0.9 copy-start.11
  12.9 0.9 copy-start.12
where the time goes:
time: 91.4 us; the launch traced here: 90.9 us
  Pallas kernels  74.2 us (81%)
  local copies, waits for them, and re-layouts  14.8 us (16%)
  other arithmetic  1.24 us (1%)
    pallas_call x1, Pallas kernels, local(): pl.pallas_call(functools.partial(kernel, names, group), out_shape=[jax.Sh...  74.2 us
    unnamed x28, local copies, waits for them, and re-layouts  13.7 us

commit v1 on v0

--- a/solution.py
+++ b/solution.py
@@ -22,7 +22,7 @@
 frames_here = 4
 modes = 44
 tiles_each = 64
-loss_lane = 64
+loss_row = 44
 
 
 def dot(a, b, precision=HIGH):
@@ -54,8 +54,24 @@
     pupil[:side, :span], pupil[:side, pad_span : pad_span + span] = c[:, rows], s[:, rows]
     pupil[side:, :span], pupil[side:, pad_span : pad_span + span] = -s[:, rows], c[:, rows]
     real = np.concatenate([c, -s], axis=0)
-    tables = (both, both.T, pupil, pupil.T, real, real.T, half_plane, half_plane.T, swapped / side)
-    return tuple(np.ascontiguousarray(t.astype(np.float32)) for t in tables)
+    narrow = np.concatenate([real, half_plane], axis=1)
+    pupil_wide = np.concatenate([pupil, np.zeros((2 * side, 2 * side - 2 * pad_span))], axis=1)
+    tables = (swapped / side, narrow, both, pupil_wide, both.T, pupil.T, real.T, half_plane.T)
+    return np.concatenate(tables).astype(np.float32)
+
+
+def split_tables(ref):
+    sizes = (256, 256, 256, 256, 256, 2 * pad_span, side, side)
+    views, at = [], 0
+    for size in sizes:
+        views.append(ref.at[at : at + size])
+        at += size
+    swapped, narrow, both, pupil, both_t, pupil_t, real_t, half_plane_t = views
+    return types.SimpleNamespace(
+        swapped=swapped, real=narrow.at[:, 0:side], half_plane=narrow.at[:, side:], both=both,
+        pupil=pupil.at[:, 0 : 2 * pad_span], both_t=both_t, pupil_t=pupil_t, real_t=real_t,
+        half_plane_t=half_plane_t,
+    )
 
 
 def aperture_area():
@@ -113,17 +129,21 @@
     return jnp.sum(value.reshape(images, tiles_each, value.shape[1]), axis=1)
 
 
-def encode(tiles, embed, first, second, head, hid_pre, inn_pre, inner_sum, pooled):
-    pre = dot(tiles[...], embed[...], HIGHEST)
-    hid_pre[...] = pre
+def encode(s):
+    s.wait("embed")
+    pre = dot(s.tiles[...], s.embed[...], HIGHEST)
+    s.hid_pre[...] = pre
     hidden = silu_act(pre)
-    pre2 = dot(hidden, first[...], HIGHEST)
-    inn_pre[...] = pre2
-    total = tile_sum(silu_act(pre2))
-    inner_sum[...] = total
-    mean = (tile_sum(hidden) + dot(total, second[...], HIGHEST)) * (1.0 / tiles_each)
-    pooled[...] = mean
-    return dot(mean, head[...], HIGHEST)
+    s.wait("first")
+    pre = dot(hidden, s.first[...], HIGHEST)
+    s.inn_pre[...] = pre
+    total = tile_sum(silu_act(pre))
+    s.inner_sum[...] = total
+    s.wait("second")
+    mean = (tile_sum(hidden) + dot(total, s.second[...], HIGHEST)) * (1.0 / tiles_each)
+    s.pooled[...] = mean
+    s.wait("head")
+    return dot_nt(mean, s.head[...], HIGHEST)
 
 
 def pupil_field(alpha, screens, spread, field):
@@ -162,23 +182,25 @@
     return edge
 
 
-def forward(img, screens, embed, first, second, head, tables, s):
-    both, _, pupil, _, real, _, half_plane, _, swapped = tables
+def forward(s, t):
+    img = s.img
     alt = alternating(1)
     slot = jnp.logical_and(
         lax.broadcasted_iota(jnp.int32, (8, 2 * side), 0) == 0,
         lax.broadcasted_iota(jnp.int32, (8, 2 * side), 1) == half,
     )
+    s.wait("img")
     cut_tiles(img, s.tiles)
-    alpha = encode(s.tiles, embed, first, second, head, s.hid_pre, s.inn_pre, s.inner_sum, s.pooled)
+    alpha = encode(s)
+    s.wait("tables")
     planes = jnp.concatenate([img[n] for n in range(images)], axis=1)
-    edge = real_transform(planes, real, swapped, s.staged, s.spec, alt)
+    edge = real_transform(planes, t.real, t.swapped, s.staged, s.spec, alt)
     for n in range(images):
         s.spec[n, 0:8, :] = jnp.where(slot, edge[n] * (1.0 / side), s.spec[n, 0:8, :])
         s.energy[n : n + 1, :] = jnp.sum(img[n] * img[n], axis=0, keepdims=True)
-    s.wait_screens()
-    pupil_field(alpha, screens, s.spread, s.field)
-    rowed = dot(s.field[...].reshape(pad_span * images, 2 * side), both[...])
+    s.wait("screens")
+    pupil_field(alpha, s.screens, s.spread, s.field)
+    rowed = dot(s.field[...].reshape(pad_span * images, 2 * side), t.both[...])
     s.rowed_r[...] = rowed[:, 0:side]
     s.rowed_i[...] = rowed[:, side : 2 * side]
     for n in range(images):
@@ -186,11 +208,11 @@
         rows = pl.ds(n, pad_span, stride=images)
         s.stack[0:pad_span, lanes] = s.rowed_r[rows, :]
         s.stack[pad_span : 2 * pad_span, lanes] = s.rowed_i[rows, :]
-    s.focal[...] = dot(pupil[...], s.stack[...])
+    s.focal[...] = dot(t.pupil[...], s.stack[...])
     scale = 1.0 / (side * side * aperture_area())
     fr, fi = s.focal[0:side, :], s.focal[side : 2 * side, :]
     spot = (fr * fr + fi * fi) * scale
-    edge = real_transform(spot, real, half_plane, s.staged, s.otf, alt)
+    edge = real_transform(spot, t.real, t.half_plane, s.staged, s.otf, alt)
     lane = lax.broadcasted_iota(jnp.int32, (side, side), 1)
     real_slot, at_corner = lane < half, corner(side)
     for n in range(images):
@@ -211,8 +233,8 @@
         s.part[p * 16 : (p + 1) * 16, 8:16, :] = den.reshape(16, 8, side)
 
 
-def backward(screens, tables, s):
-    _, both_t, _, pupil_t, _, real_t, _, half_plane_t, _ = tables
+def backward(s, t):
+    screens = s.screens
     lane = lax.broadcasted_iota(jnp.int32, (side, side), 1)
     real_slot, at_corner = lane < half, corner(side)
     alt = alternating(1)
@@ -236,20 +258,20 @@
             n = p * frames_here + f
             lanes = slice(n * side, (n + 1) * side)
             g = a * s.spec[n, :, 0:side] + b * s.spec[n, :, side : 2 * side] + m * s.otf[n]
-            y = dot(g, half_plane_t[...])
+            y = dot(g, t.half_plane_t[...])
             s.staged[0:side, lanes] = y[:, 0:side]
             s.staged[side : 2 * side, lanes] = y[:, side : 2 * side]
             s.staged[0:1, lanes] = y[0:1, 0:side] + g[0:1, half : half + 1] * alt
-    d_spot = dot(real_t[...], s.staged[...]) * (2.0 / (side * side * aperture_area()))
+    d_spot = dot(t.real_t[...], s.staged[...]) * (2.0 / (side * side * aperture_area()))
     d_focal = jnp.concatenate([s.focal[0:side, :] * d_spot, s.focal[side : 2 * side, :] * d_spot], axis=0)
-    s.stack[...] = dot(pupil_t[...], d_focal)
+    s.stack[...] = dot(t.pupil_t[...], d_focal)
     for n in range(images):
         lanes = slice(n * side, (n + 1) * side)
         rows = pl.ds(n, pad_span, stride=images)
         s.rowed_r[rows, :] = s.stack[0:pad_span, lanes]
         s.rowed_i[rows, :] = s.stack[pad_span : 2 * pad_span, lanes]
     rowed = jnp.concatenate([s.rowed_r[...], s.rowed_i[...]], axis=1)
-    d_field = dot(rowed, both_t[...]).reshape(pad_span, images, 2 * side)
+    d_field = dot(rowed, t.both_t[...]).reshape(pad_span, images, 2 * side)
     f_r, f_i = s.field[:, :, 0:side], s.field[:, :, side : 2 * side]
     s.phase[...] = d_field[:, :, side : 2 * side] * f_r - d_field[:, :, 0:side] * f_i
 
@@ -275,21 +297,20 @@
     return d_alpha, losses
 
 
-def encoder_gradients(d_alpha, tiles, embed, first, second, head, s):
-    d_alpha44 = d_alpha[:, 0:modes]
-    d_pooled = dot_nt(d_alpha44, head[...]) * (1.0 / tiles_each)
-    s.grad_head[:, 0:side] = dot_tn(s.pooled[...], d_alpha)
+def encoder_gradients(d_alpha, s):
+    d_pooled = dot(d_alpha[:, 0:modes], s.head[...]) * (1.0 / tiles_each)
+    s.grad_tail[...] = dot_tn(d_alpha, s.pooled[...])
     s.grad_second[...] = dot_tn(s.inner_sum[...], d_pooled)
-    d_inner = dot_nt(d_pooled, second[...])
-    width = embed.shape[1]
+    d_inner = dot_nt(d_pooled, s.second[...])
+    width = s.embed.shape[1]
 
     def spread(value):
         return jnp.broadcast_to(value[:, None, :], (images, tiles_each, width)).reshape(-1, width)
 
     d_inner_pre = spread(d_inner) * silu_slope(s.inn_pre[...])
     s.grad_first[...] = dot_tn(silu_act(s.hid_pre[...]), d_inner_pre)
-    d_hidden = spread(d_pooled) + dot_nt(d_inner_pre, first[...])
-    s.grad_embed[...] = dot_tn(tiles[...], d_hidden * silu_slope(s.hid_pre[...]))
+    d_hidden = spread(d_pooled) + dot_nt(d_inner_pre, s.first[...])
+    s.grad_embed[...] = dot_tn(s.tiles[...], d_hidden * silu_slope(s.hid_pre[...]))
 
 
 state_shapes = dict(
@@ -313,9 +334,15 @@
     ratio=(32, 8, side),
     phase=(pad_span, images, side),
     screens=(modes, span * side),
+    img=(images, side, side),
+    embed=(256, 256),
+    first=(256, 256),
+    second=(256, 256),
+    head=(modes, 256),
+    tables=(1680, 256),
 )
 gradient_shapes = dict(
-    grad_embed=(256, 256), grad_first=(256, 256), grad_second=(256, 256), grad_head=(256, side), grad_tail=(128, 256)
+    grad_embed=(256, 256), grad_first=(256, 256), grad_second=(256, 256), grad_tail=(128, 256)
 )
 
 
@@ -550,32 +577,36 @@
         one.wait_send()
 
 
+operands = ("img", "embed", "first", "second", "head", "tables", "screens")
+
+
 def kernel(names, group, *refs):
-    img, screens_hbm, embed, first, second, head = refs[:6]
-    tables, (alpha_ref, total_ref), scratch = refs[6:15], refs[15:17], refs[17:]
+    sources, (alpha_ref, total_ref), scratch = refs[:7], refs[7:9], refs[9:]
     s = types.SimpleNamespace(**dict(zip(names, scratch)))
     buffers = scratch[len(names) : -3]
-    screens_sem, spectral_sems, gradient_sems = scratch[-3:]
+    fetch_sems, spectral_sems, gradient_sems = scratch[-3:]
+    fetches = {}
+    for i, name in enumerate(operands):
+        source = sources[i]
+        if name == "screens":
+            source = source.at[:, pl.ds(half // 2 * side, span * side)]
+        fetches[name] = pltpu.make_async_copy(source, getattr(s, name), fetch_sems.at[i])
+        fetches[name].start()
+    s.wait = lambda name: fetches[name].wait()
     greeted = greet(group)
-    fetch = pltpu.make_async_copy(
-        screens_hbm.at[:, pl.ds(half // 2 * side, span * side)], s.screens, screens_sem
-    )
-    fetch.start()
-    s.wait_screens = fetch.wait
-    forward(img, s.screens, embed, first, second, head, tables, s)
+    t = split_tables(s.tables)
+    forward(s, t)
     pl.semaphore_wait(pltpu.get_barrier_semaphore(), greeted)
     spectral_exchange(s, group, spectral_sems)
-    d_alpha, losses = backward(s.screens, tables, s)
+    d_alpha, losses = backward(s, t)
     alpha_ref[...] = d_alpha
-    encoder_gradients(d_alpha, s.tiles, embed, first, second, head, s)
-    s.grad_tail[:, 0:side] = s.grad_head[0:side, :]
-    s.grad_tail[:, side : 2 * side] = s.grad_head[side : 2 * side, :]
+    encoder_gradients(d_alpha, s)
     lane = lax.broadcasted_iota(jnp.int32, (1, side), 1)
-    top = s.grad_tail[0:1, 0:side]
+    row = jnp.zeros((1, side), jnp.float32)
     for p in range(len(losses)):
-        at = loss_lane + lax.axis_index("dp") * len(losses) + p
-        top = jnp.where(lane == at, losses[p], top)
-    s.grad_tail[0:1, 0:side] = top
+        at = lax.axis_index("dp") * len(losses) + p
+        row = jnp.where(lane == at, losses[p], row)
+    s.grad_tail[loss_row : loss_row + 1, 0:side] = row
     parts = (s.grad_embed, s.grad_first, s.grad_second, s.grad_tail)
     gradient_exchange(parts, total_ref, buffers, gradient_sems)
 
@@ -593,30 +624,29 @@
             jax.ShapeDtypeStruct((images, side), f32),
             jax.ShapeDtypeStruct((sum(part_rows), 2 * side), f32),
         ],
-        in_specs=[vmem, pl.BlockSpec(memory_space=pl.ANY)] + [vmem] * 13,
+        in_specs=[pl.BlockSpec(memory_space=pltpu.HBM)] * len(operands),
         out_specs=[vmem] * 2,
         scratch_shapes=[pltpu.VMEM(shape, f32) for shape in shapes]
         + [
-            pltpu.SemaphoreType.DMA(()),
+            pltpu.SemaphoreType.DMA((len(operands),)),
             pltpu.SemaphoreType.DMA((4, group)),
             pltpu.SemaphoreType.DMA((2, 64)),
         ],
         compiler_params=pltpu.CompilerParams(
-            collective_id=0, has_side_effects=True, vmem_limit_bytes=48 << 20
+            collective_id=0, has_side_effects=True, vmem_limit_bytes=63 << 20
         ),
     )(
         recorded_exposures.reshape(images, side, side),
-        screens, embed, first, second, head, *transform_tables(),
+        embed, first, second, head.T, transform_tables(), screens,
     )
-    tail = total[768:]
-    start = loss_lane + lax.axis_index("dp") * regions
-    losses = lax.dynamic_slice(tail, (0, start), (1, regions))[0]
+    start = lax.axis_index("dp") * regions
+    losses = lax.dynamic_slice(total, (768 + loss_row, start), (1, regions))[0]
     return (
         d_alpha[:, :modes].reshape(regions, -1, modes),
         total[:256],
         total[256:512],
         total[512:768],
-        jnp.concatenate([tail[:, :modes], tail[:, side : side + modes]], axis=0),
+        total[768 : 768 + modes].T,
         losses / (group * frames_here),
     )
 

time: 91.4 us -> 82.8 us (0.906)
  local copies, waits for them, and re-layouts: 14.8 us -> 4.69 us
  Pallas kernels: 74.2 us -> 76 us
    unnamed x28 -> x1, local copies, waits for them, and re-layouts: 13.7 us -> 1.27 us
    pallas_call x1, Pallas kernels: 74.2 us -> 76 us  [local(): pl.pallas_call(functools.partial(kernel, names, group), out_shape=[jax.Sh...]
    transpose x0 -> x1, local copies, waits for them, and re-layouts: none -> 1.42 us  [local(): total[768:768 + modes]]
    slice x1, local copies, waits for them, and re-layouts: 0.89 us -> 2 us  [local(): total[512:768]]
where the time goes in v1:
time: 82.8 us; the launch traced here: 82.6 us
  Pallas kernels  76 us (92%)
  local copies, waits for them, and re-layouts  4.69 us (6%)
  other arithmetic  1.26 us (2%)
    pallas_call x1, Pallas kernels, local(): pl.pallas_call(functools.partial(kernel, names, group), out_shape=[jax.Sh...  76 us
    slice x1, local copies, waits for them, and re-layouts, local(): total[512:768]  2 us

profile of v1, /device:TPU:1, one launch (start us, length us, event | category | flops | bytes accessed | tf_op | source)
XLA Modules:
  0.0 82.6 jit_solution(9048625425398734680)
XLA Ops:
  0.6 76.0 %shard_map.118 = (f32[8,128]{1,0:T(8,128)}, f32[896,256]{1,0:T(8,128)}) custom-call(f32[8,128,128]{2,1,0:T(8,128)} %bitcast.8, f32[256,256]{1,0:T(8,128)} %refs_1_.1, f32[256,256]{1,0:T(8,128)} %refs_2_.1, f32[256,256]{1,0:T(8,128)} %refs_3_.1, f32[44,256]{1,0:T(8,128)} %bitcast.9, f32[1680,256]{1,0:T(8,128)} %constant.19.clone.refs_5_, f32[44,16384]{1,0:T(8,128)} %refs_6_.1), custom_call_target="tpu_custom_call" | custom-call | tf_op jit(solution)/shard_map/pallas_call | solution.py:621
  76.7 1.3 %multiply_bitcast_fusion = f32[2]{0:T(128)} fusion(f32[896,256]{1,0:T(8,128)} %get-tuple-element.9, s32[]{:T(128)S(6)} %select_n.3), kind=kLoop, calls=%fused_computation.1 | loop fusion | flops 2 | bytes 20 | tf_op jit(solution)/shard_map/div | solution.py:650
  77.9 1.4 %slice_bitcast_fusion = f32[256,44]{0,1:T(8,128)} fusion(f32[896,256]{1,0:T(8,128)} %get-tuple-element.9), kind=kLoop, calls=%fused_computation | loop fusion | bytes 90112 | tf_op jit(solution)/shard_map/transpose | solution.py:649
  79.3 2.0 %fusion = (f32[256,256]{1,0:T(8,128)}, f32[256,256]{1,0:T(8,128)}, f32[256,256]{1,0:T(8,128)}) fusion(f32[896,256]{1,0:T(8,128)} %get-tuple-element.9), kind=kLoop, calls=%fused_computation.2 | loop fusion | bytes 1572864 | tf_op jit(solution)/shard_map/slice | solution.py:648
  81.3 1.3 %copy.14 = f32[2,4,44]{2,1,0:T(4,128)} copy(f32[2,4,44]{2,1,0:T(4,128)} %bitcast.10) | data formatting | bytes 2816

commit v2 on v1

v2 whole, which is shorter than its diff:
```python
import functools
import types

import jax
import jax.numpy as jnp
import numpy as np
from jax import lax
from jax.experimental import pallas as pl
from jax.experimental.pallas import tpu as pltpu
from jax.sharding import PartitionSpec as P

entry_block_length = 16
regularizer_relative = 0.001
MESH = pl.DeviceIdType.MESH
HIGH = lax.Precision.HIGH
HIGHEST = lax.Precision.HIGHEST
side = 128
half = side // 2
span = half + 1
pad_span = 72
images = 8
frames_here = 4
modes = 44
tiles_each = 64
loss_row = 44


def dot(a, b, precision=HIGH):
    return jnp.dot(a, b, precision=precision, preferred_element_type=jnp.float32)


def dot_tn(a, b, precision=HIGH):
    return lax.dot_general(
        a, b, (((0,), (0,)), ((), ())), precision=precision, preferred_element_type=jnp.float32
    )


def dot_nt(a, b, precision=HIGH):
    return lax.dot_general(
        a, b, (((1,), (1,)), ((), ())), precision=precision, preferred_element_type=jnp.float32
    )


def transform_tables():
    index = np.arange(side)
    angle = 2.0 * np.pi / side * (index[:, None] * index[None, :] % side)
    c, s = np.cos(angle), np.sin(angle)
    both = np.block([[c, -s], [s, c]])
    lo = slice(0, half)
    half_plane = np.concatenate([both[:, lo], both[:, side : side + half]], axis=1)
    swapped = np.concatenate([half_plane, half_plane[:, half:], half_plane[:, :half]], axis=1)
    rows = slice(half // 2, half // 2 + span)
    pupil = np.zeros((2 * side, 2 * pad_span))
    pupil[:side, :span], pupil[:side, pad_span : pad_span + span] = c[:, rows], s[:, rows]
    pupil[side:, :span], pupil[side:, pad_span : pad_span + span] = -s[:, rows], c[:, rows]
    real = np.concatenate([c, -s], axis=0)
    narrow = np.concatenate([real, half_plane], axis=1)
    pupil_wide = np.concatenate([pupil, np.zeros((2 * side, 2 * side - 2 * pad_span))], axis=1)
    tables = (swapped / side, narrow, both, pupil_wide, both.T, pupil.T, real.T, half_plane.T)
    return np.concatenate(tables).astype(np.float32)


def split_tables(ref):
    sizes = (256, 256, 256, 256, 256, 2 * pad_span, side, side)
    views, at = [], 0
    for size in sizes:
        views.append(ref.at[at : at + size])
        at += size
    swapped, narrow, both, pupil, both_t, pupil_t, real_t, half_plane_t = views
    return types.SimpleNamespace(
        swapped=swapped, real=narrow.at[:, 0:side], half_plane=narrow.at[:, side:], both=both,
        pupil=pupil.at[:, 0 : 2 * pad_span], both_t=both_t, pupil_t=pupil_t, real_t=real_t,
        half_plane_t=half_plane_t,
    )


def aperture_area():
    at = np.arange(side) - half
    return float(np.sum(at[:, None] ** 2 + at[None, :] ** 2 <= (side // 4) ** 2))


def sigmoid(value):
    return 1.0 / (1.0 + jnp.exp(-value))


def silu_act(value):
    return value / (1.0 + jnp.exp(-value))


def silu_slope(value):
    gate = sigmoid(value)
    return gate * (1.0 + value * (1.0 - gate))


def alternating(rows):
    lane = lax.broadcasted_iota(jnp.int32, (rows, side), 1)
    return jnp.where(lax.rem(lane, 2) == 0, 1.0, -1.0).astype(jnp.float32)


def corner(rows):
    row = lax.broadcasted_iota(jnp.int32, (rows, side), 0)
    lane = lax.broadcasted_iota(jnp.int32, (rows, side), 1)
    return jnp.logical_and(row == 0, lax.rem(lane, half) == 0)


def cut_tiles(img, tiles):
    group = lax.broadcasted_iota(jnp.int32, (8, side), 1) // 16

    def one(n, carry):
        for g in range(2):
            x = [img[n, pl.ds(8 * g + j, 8, stride=16), :] for j in range(8)]
            for bit in (1, 2, 4):
                low = lax.rem(group // bit, 2) == 0
                y = list(x)
                for p in range(8):
                    if p & bit == 0:
                        q = p + bit
                        y[p] = jnp.where(low, x[p], pltpu.roll(x[q], 16 * bit, 1))
                        y[q] = jnp.where(low, pltpu.roll(x[p], side - 16 * bit, 1), x[q])
                x = y
            for c in range(8):
                tiles[pl.ds(pl.multiple_of(n * 64 + c * 8, 8), 8), g * side : (g + 1) * side] = x[c]
        return carry

    lax.fori_loop(0, images, one, 0)


def tile_sum(value):
    return jnp.sum(value.reshape(images, tiles_each, value.shape[1]), axis=1)


def encode(s):
    s.wait("embed")
    pre = dot(s.tiles[...], s.embed[...], HIGHEST)
    s.hid_pre[...] = pre
    hidden = silu_act(pre)
    s.wait("first")
    pre = dot(hidden, s.first[...], HIGHEST)
    s.inn_pre[...] = pre
    total = tile_sum(silu_act(pre))
    s.inner_sum[...] = total
    s.wait("second")
    mean = (tile_sum(hidden) + dot(total, s.second[...], HIGHEST)) * (1.0 / tiles_each)
    s.pooled[...] = mean
    s.wait("head")
    return dot_nt(mean, s.head[...], HIGHEST)


def pupil_field(alpha, screens, spread, field):
    for m in range(modes):
        spread[m] = jnp.broadcast_to(alpha[:, m : m + 1], (images, side))
    lane = lax.broadcasted_iota(jnp.int32, (images, side), 1) - half
    width = 5

    def rows(block, carry):
        at = [pl.multiple_of((block * width + i) * side, side) for i in range(width)]
        total = [jnp.zeros((images, side), jnp.float32) for _ in range(width)]
        for m in range(modes):
            weight = spread[m]
            for i in range(width):
                total[i] = total[i] + weight * screens[m : m + 1, pl.ds(at[i], side)]
        for i in range(width):
            up = block * width + i - half // 2
            inside = lane * lane + up * up <= (side // 4) ** 2
            field[block * width + i, :, 0:side] = jnp.where(inside, jnp.cos(total[i]), 0.0)
            field[block * width + i, :, side : 2 * side] = jnp.where(inside, jnp.sin(total[i]), 0.0)
        return carry

    lax.fori_loop(0, span // width, rows, 0)
    for i in range(span, pad_span):
        field[i] = jnp.zeros((images, 2 * side), jnp.float32)


def patch_lanes(p):
    return slice(p * frames_here * side, (p + 1) * frames_here * side)


def real_transform(planes, first_table, second_table, s, p, out):
    lanes = patch_lanes(p)
    s.staged[:, lanes] = dot(first_table[...], planes)
    edge = []
    for n in range(p * frames_here, (p + 1) * frames_here):
        lanes = slice(n * side, (n + 1) * side)
        edge.append(jnp.sum(s.staged[0:1, lanes] * alternating(1), axis=1, keepdims=True))
        pair = jnp.concatenate([s.staged[0:side, lanes], s.staged[side : 2 * side, lanes]], axis=1)
        out[n] = dot(pair, second_table[...])
    return edge


def edge_slot(width):
    row = lax.broadcasted_iota(jnp.int32, (8, width), 0)
    lane = lax.broadcasted_iota(jnp.int32, (8, width), 1)
    return jnp.logical_and(row == 0, lane == half)


def frame_spectra(s, t, p):
    here = range(p * frames_here, (p + 1) * frames_here)
    planes = jnp.concatenate([s.img[n] for n in here], axis=1)
    edge = real_transform(planes, t.real, t.swapped, s, p, s.spec)
    for n in here:
        value = edge[n - here[0]] * (1.0 / side)
        s.spec[n, 0:8, :] = jnp.where(edge_slot(2 * side), value, s.spec[n, 0:8, :])


def frame_energy(s):
    for n in range(images):
        s.energy[n : n + 1, :] = jnp.sum(s.img[n] * s.img[n], axis=0, keepdims=True)


def pupil_rows(s, t):
    rowed = dot(s.field[...].reshape(pad_span * images, 2 * side), t.both[...])
    s.rowed_r[...] = rowed[:, 0:side]
    s.rowed_i[...] = rowed[:, side : 2 * side]
    for n in range(images):
        lanes = slice(n * side, (n + 1) * side)
        rows = pl.ds(n, pad_span, stride=images)
        s.stack[0:pad_span, lanes] = s.rowed_r[rows, :]
        s.stack[pad_span : 2 * pad_span, lanes] = s.rowed_i[rows, :]


def spectral_sums(s, t, p):
    lanes = patch_lanes(p)
    s.focal[:, lanes] = dot(t.pupil[...], s.stack[:, lanes])
    fr, fi = s.focal[0:side, lanes], s.focal[side : 2 * side, lanes]
    spot = (fr * fr + fi * fi) * (1.0 / (side * side * aperture_area()))
    edge = real_transform(spot, t.real, t.half_plane, s, p, s.otf)
    real_slot = lax.broadcasted_iota(jnp.int32, (side, side), 1) < half
    at_corner = corner(side)
    t1 = t2 = t3 = 0.0
    for f in range(frames_here):
        n = p * frames_here + f
        s.otf[n, 0:8, :] = jnp.where(edge_slot(side), edge[f], s.otf[n, 0:8, :])
        o, a, b = s.otf[n], s.spec[n, :, 0:side], s.spec[n, :, side : 2 * side]
        t1, t2, t3 = t1 + a * o, t2 + b * o, t3 + o * o
    turned = pltpu.roll(t2, half, 1)
    num = jnp.where(real_slot, t1 + pltpu.roll(t1, half, 1), turned - t2)
    num = jnp.where(at_corner, t1, num)
    den = jnp.where(at_corner, t3, t3 + pltpu.roll(t3, half, 1))
    s.part[p * 16 : (p + 1) * 16, 0:8, :] = num.reshape(16, 8, side)
    s.part[p * 16 : (p + 1) * 16, 8:16, :] = den.reshape(16, 8, side)


def total_of(value):
    return jnp.sum(jnp.sum(value, axis=0, keepdims=True), axis=1, keepdims=True)


def focal_adjoint(s, t, p):
    lane = lax.broadcasted_iota(jnp.int32, (side, side), 1)
    real_slot, at_corner = lane < half, corner(side)
    per_pixel = 1.0 / (side * side)
    weight = jnp.where(lax.rem(lane, half) == 0, per_pixel, 2.0 * per_pixel)
    rho = s.ratio[p * 16 : (p + 1) * 16].reshape(side, side)
    num = s.part[p * 16 : (p + 1) * 16, 0:8, :].reshape(side, side)
    turned = pltpu.roll(rho, half, 1)
    square = rho * rho
    a = jnp.where(jnp.logical_or(real_slot, at_corner), rho, turned) * (-2.0 * weight)
    b = jnp.where(real_slot, turned, -rho)
    b = jnp.where(at_corner, 0.0, b) * (-2.0 * weight)
    m = jnp.where(at_corner, square, square + turned * turned) * (2.0 * weight)
    energy = total_of(s.energy[p * frames_here : (p + 1) * frames_here, :])
    loss = energy * per_pixel - total_of(weight * rho * num)
    for f in range(frames_here):
        n = p * frames_here + f
        lanes = slice(n * side, (n + 1) * side)
        g = a * s.spec[n, :, 0:side] + b * s.spec[n, :, side : 2 * side] + m * s.otf[n]
        y = dot(g, t.half_plane_t[...])
        s.staged[0:side, lanes] = y[:, 0:side]
        s.staged[side : 2 * side, lanes] = y[:, side : 2 * side]
        s.staged[0:1, lanes] = y[0:1, 0:side] + g[0:1, half : half + 1] * alternating(1)
    lanes = patch_lanes(p)
    d_spot = dot(t.real_t[...], s.staged[:, lanes]) * (2.0 / (side * side * aperture_area()))
    d_focal = jnp.concatenate(
        [s.focal[0:side, lanes] * d_spot, s.focal[side : 2 * side, lanes] * d_spot], axis=0
    )
    s.stack[:, lanes] = dot(t.pupil_t[...], d_focal)
    return loss


def alpha_adjoint(s, t):
    screens = s.screens
    for n in range(images):
        lanes = slice(n * side, (n + 1) * side)
        rows = pl.ds(n, pad_span, stride=images)
        s.rowed_r[rows, :] = s.stack[0:pad_span, lanes]
        s.rowed_i[rows, :] = s.stack[pad_span : 2 * pad_span, lanes]
    rowed = jnp.concatenate([s.rowed_r[...], s.rowed_i[...]], axis=1)
    d_field = dot(rowed, t.both_t[...]).reshape(pad_span, images, 2 * side)
    f_r, f_i = s.field[:, :, 0:side], s.field[:, :, side : 2 * side]
    s.phase[...] = d_field[:, :, side : 2 * side] * f_r - d_field[:, :, 0:side] * f_i

    alpha_lane = lax.broadcasted_iota(jnp.int32, (images, side), 1)
    d_alpha = jnp.zeros((images, side), jnp.float32)
    chunk = 11
    for start in range(0, modes, chunk):

        def rows(i, total, start=start):
            value = s.phase[i]
            at = pl.multiple_of(i * side, side)
            return tuple(
                total[m] + value * screens[start + m : start + m + 1, pl.ds(at, side)]
                for m in range(chunk)
            )

        zero = tuple(jnp.zeros((images, side), jnp.float32) for _ in range(chunk))
        total = lax.fori_loop(0, span, rows, zero)
        for m in range(chunk):
            d_alpha = jnp.where(
                alpha_lane == start + m, jnp.sum(total[m], axis=1, keepdims=True), d_alpha
            )
    return d_alpha


def spread(value):
    return jnp.broadcast_to(value[:, None, :], (images, tiles_each, 256)).reshape(-1, 256)


def gradients_after_mean(s, d_alpha):
    s.grad_tail[...] = dot_tn(d_alpha, s.pooled[...])
    d_pooled = dot(d_alpha[:, 0:modes], s.head[...]) * (1.0 / tiles_each)
    s.grad_second[...] = dot_tn(s.inner_sum[...], d_pooled)
    return d_pooled


def gradient_first(s, d_pooled):
    d_inner = spread(dot_nt(d_pooled, s.second[...])) * silu_slope(s.inn_pre[...])
    s.grad_first[...] = dot_tn(silu_act(s.hid_pre[...]), d_inner)
    return d_inner


def gradient_embed(s, d_pooled, d_inner):
    d_hidden = spread(d_pooled) + dot_nt(d_inner, s.first[...])
    s.grad_embed[...] = dot_tn(s.tiles[...], d_hidden * silu_slope(s.hid_pre[...]))


state_shapes = dict(
    tiles=(images * tiles_each, 256),
    hid_pre=(images * tiles_each, 256),
    inn_pre=(images * tiles_each, 256),
    inner_sum=(images, 256),
    pooled=(images, 256),
    energy=(images, side),
    spread=(modes, images, side),
    field=(pad_span, images, 2 * side),
    rowed_r=(pad_span * images, side),
    rowed_i=(pad_span * images, side),
    stack=(2 * pad_span, images * side),
    focal=(2 * side, images * side),
    staged=(2 * side, images * side),
    spec=(images, side, 2 * side),
    otf=(images, side, side),
    part=(32, 16, side),
    core_part=(16, 16, side),
    merged=(16, 16, side),
    inbox=(15, 16, side),
    ratio=(32, 8, side),
    phase=(pad_span, images, side),
    screens=(modes, span * side),
    img=(images, side, side),
    embed=(256, 256),
    first=(256, 256),
    second=(256, 256),
    head=(modes, 256),
    tables=(1680, 256),
)
gradient_shapes = dict(
    grad_embed=(256, 256), grad_first=(256, 256), grad_second=(256, 256), grad_tail=(128, 256)
)


def ring_distance(step, size):
    return min(step, size - step)


plane_steps = sorted(
    ((dx, dy) for dx in range(4) for dy in range(4) if dx or dy),
    key=lambda d: ring_distance(d[0], 4) + ring_distance(d[1], 4),
)
burst_steps = sorted(
    ((dx, dz) for dx in range(4) for dz in range(4) if dx or dz),
    key=lambda d: ring_distance(d[0], 4) + 2 * ring_distance(d[1], 4),
)
column_steps = sorted(range(1, 8), key=lambda d: ring_distance(d, 8))


class Place:
    def __init__(self):
        self.dp, self.frame = lax.axis_index("dp"), lax.axis_index("frame")
        self.core, self.x = lax.rem(self.frame, 2), lax.rem(self.frame // 2, 4)
        self.y, self.z_lo = self.dp // 2, lax.rem(self.dp, 2)
        self.z_hi = self.frame // 8
        self.z = self.z_hi * 2 + self.z_lo
        self.spot = self.x * 4 + self.y
        self.seat = self.z_hi * 4 + self.x

    def device(self, core, x, y, z):
        return {"dp": y * 2 + lax.rem(z, 2), "frame": (z // 2) * 8 + x * 2 + core}

    def sibling(self):
        return self.device(1 - self.core, self.x, self.y, self.z)

    def plane(self, step, sign=1):
        x = lax.rem(self.x + 4 + sign * step[0], 4)
        y = lax.rem(self.y + 4 + sign * step[1], 4)
        return x * 4 + y, self.device(self.core, x, y, self.z)

    def burst(self, step, sign=1):
        x = lax.rem(self.x + 4 + sign * step[0], 4)
        z_hi = lax.rem(self.z_hi + 4 + sign * step[1], 4)
        return z_hi * 4 + x, self.device(self.core, x, self.y, z_hi * 2 + self.z_lo)

    def column(self, step):
        return self.device(self.core, self.x, self.y, lax.rem(self.z + step, 8))


def greet():
    place = Place()
    targets = [place.sibling()]
    targets += [place.burst(step)[1] for step in burst_steps]
    targets += [place.plane(step)[1] for step in plane_steps if step[1]]
    targets += [place.column(step) for step in column_steps if step % 2]
    for target in targets:
        pl.semaphore_signal(
            pltpu.get_barrier_semaphore(), inc=1, device_id=target, device_id_type=MESH
        )
    return len(targets)


class Mail:
    def __init__(self, sems):
        self.sems, self.used, self.sent = sems, 0, []

    def send(self, src, dst, target):
        slot = self.used
        self.used += 1
        copy = pltpu.make_async_remote_copy(
            src_ref=src,
            dst_ref=dst,
            send_sem=self.sems.at[0, slot],
            recv_sem=self.sems.at[1, slot],
            device_id=target,
            device_id_type=MESH,
        )
        copy.start()
        self.sent.append(copy)
        return copy

    def finish(self):
        for copy in self.sent:
            copy.wait_send()


def spectral_exchange(s, regularizer_strength, sems):
    place, mail = Place(), Mail(sems)
    core, seat = place.core, place.seat
    swap = mail.send(s.part.at[pl.ds((1 - core) * 16, 16)], s.core_part, place.sibling())
    swap.wait_recv()
    s.merged[...] = s.part[pl.ds(core * 16, 16)] + s.core_part[...]
    copies = {}
    for i, step in reversed(list(enumerate(burst_steps))):
        there, device = place.burst(step)
        copies[i] = mail.send(s.merged.at[there], s.inbox.at[i], device)
    total = s.merged[seat]
    for i in range(len(burst_steps)):
        copies[i].wait_recv()
        total = total + s.inbox[i]
    mine = core * 16 + seat
    s.ratio[mine] = total[0:8] / (total[8:16] + regularizer_strength)
    copies = {}
    for i, step in reversed(list(enumerate(burst_steps))):
        copies[i] = mail.send(s.ratio.at[mine], s.ratio.at[mine], place.burst(step)[1])
    passed = [mail.send(s.ratio.at[mine], s.ratio.at[mine], place.sibling())]
    for i, step in enumerate(burst_steps):
        copies[i].wait_recv()
        came = core * 16 + place.burst(step, -1)[0]
        passed.append(mail.send(s.ratio.at[came], s.ratio.at[came], place.sibling()))
    for copy in passed:
        copy.wait_recv()
    mail.finish()


class GradientGroup:
    def __init__(self, parts, buffers, sems):
        self.parts = parts
        self.core_in, self.sums, self.inbox, self.column_in, self.full, self.other = buffers
        self.place, self.mail = Place(), Mail(sems)
        core = self.place.core
        self.mine = pl.ds(pl.multiple_of(core * side, side), side)
        self.theirs = pl.ds(pl.multiple_of((1 - core) * side, side), side)
        self.swaps = []

    def send_core(self, part):
        ref, at = self.parts[part]
        rows = ref.shape[0]
        self.swaps.append(
            self.mail.send(
                ref.at[:, self.theirs], self.core_in.at[at : at + rows], self.place.sibling()
            )
        )

    def send_plane(self):
        row = 0
        for swap, (ref, at) in zip(self.swaps, self.parts):
            swap.wait_recv()
            rows = ref.shape[0]
            total = ref[:, self.mine] + self.core_in[at : at + rows]
            each = rows // 16
            self.sums[:, row : row + each, :] = total.reshape(16, each, side)
            row += each
        self.copies = {}
        for i, step in reversed(list(enumerate(plane_steps))):
            there, device = self.place.plane(step)
            self.copies[i] = self.mail.send(self.sums.at[there], self.inbox.at[i], device)

    def send_column(self):
        total = self.sums[self.place.spot]
        for i in range(len(plane_steps)):
            self.copies[i].wait_recv()
            total = total + self.inbox[i]
        z = self.place.z
        self.column_in[z] = total
        self.copies = [
            self.mail.send(self.column_in.at[z], self.column_in.at[z], self.place.column(step))
            for step in reversed(column_steps)
        ]

    def send_back(self):
        for copy in self.copies:
            copy.wait_recv()
        total = self.column_in[0]
        for z in range(1, 8):
            total = total + self.column_in[z]
        spot = self.place.spot
        self.full[spot] = total
        self.copies = {}
        for i, step in reversed(list(enumerate(plane_steps))):
            device = self.place.plane(step)[1]
            self.copies[i] = self.mail.send(self.full.at[spot], self.full.at[spot], device)
        self.passed = [
            self.mail.send(self.full.at[spot], self.other.at[spot], self.place.sibling())
        ]

    def pass_on(self):
        for i, step in enumerate(plane_steps):
            self.copies[i].wait_recv()
            came = self.place.plane(step, -1)[0]
            self.passed.append(
                self.mail.send(self.full.at[came], self.other.at[came], self.place.sibling())
            )

    def finish(self, outs):
        for copy in self.passed:
            copy.wait_recv()
        row = 0
        for (ref, _), out in zip(self.parts, outs):
            each = ref.shape[0] // 16
            for values, lanes in ((self.full, self.mine), (self.other, self.theirs)):
                out[:, lanes] = values[:, row : row + each, :].reshape(16 * each, side)
            row += each
        self.mail.finish()


def group_buffers(rows):
    each = rows // 16
    return [
        (rows, side), (16, each, side), (15, each, side), (8, each, side), (16, each, side),
        (16, each, side),
    ]


operands = ("img", "embed", "first", "second", "head", "tables", "screens")
early_rows = (256, 128)
late_rows = (256, 256)


def kernel(names, frames_total, *refs):
    sources, (alpha_ref, loss_ref, total_ref), scratch = refs[:7], refs[7:10], refs[10:]
    s = types.SimpleNamespace(**dict(zip(names, scratch)))
    buffers = scratch[len(names) : -4]
    fetch_sems, spectral_sems, early_sems, late_sems = scratch[-4:]
    fetches = {}
    for i, name in enumerate(operands):
        source = sources[i]
        if name == "screens":
            source = source.at[:, pl.ds(half // 2 * side, span * side)]
        fetches[name] = pltpu.make_async_copy(source, getattr(s, name), fetch_sems.at[i])
        fetches[name].start()
    s.wait = lambda name: fetches[name].wait()
    greeted = greet()
    t = split_tables(s.tables)

    s.wait("img")
    cut_tiles(s.img, s.tiles)
    alpha = encode(s)
    s.wait("screens")
    pupil_field(alpha, s.screens, s.spread, s.field)
    s.wait("tables")
    pupil_rows(s, t)
    patches = range(images // frames_here)
    for p in patches:
        frame_spectra(s, t, p)
        spectral_sums(s, t, p)
    frame_energy(s)
    pl.semaphore_wait(pltpu.get_barrier_semaphore(), greeted)
    spectral_exchange(s, regularizer_relative * frames_total, spectral_sems)
    losses = [focal_adjoint(s, t, p) for p in patches]
    d_alpha = alpha_adjoint(s, t)
    alpha_ref[...] = d_alpha

    early = GradientGroup(((s.grad_second, 0), (s.grad_tail, 256)), buffers[:6], early_sems)
    late = GradientGroup(((s.grad_first, 0), (s.grad_embed, 256)), buffers[6:], late_sems)
    d_pooled = gradients_after_mean(s, d_alpha)
    lane = lax.broadcasted_iota(jnp.int32, (1, side), 1)
    row = jnp.zeros((1, side), jnp.float32)
    for p in patches:
        at = lax.axis_index("dp") * len(patches) + p
        row = jnp.where(lane == at, losses[p], row)
    s.grad_tail[loss_row : loss_row + 1, 0:side] = row
    early.send_core(0)
    early.send_core(1)
    d_inner = gradient_first(s, d_pooled)
    late.send_core(0)
    early.send_plane()
    gradient_embed(s, d_pooled, d_inner)
    late.send_core(1)
    late.send_plane()
    early.send_column()
    late.send_column()
    early.send_back()
    late.send_back()
    early.pass_on()
    late.pass_on()
    early.finish((total_ref.at[512:768], total_ref.at[768:896]))
    late.finish((total_ref.at[256:512], total_ref.at[0:256]))
    at = 768 + loss_row
    loss_ref[...] = total_ref[at : at + 1, 0:side] * (1.0 / frames_total)


def local(recorded_exposures, screens, embed, first, second, head):
    regions = recorded_exposures.shape[0]
    frames_total = recorded_exposures.shape[1] * lax.axis_size("frame")
    f32 = jnp.float32
    names = list(state_shapes) + list(gradient_shapes)
    shapes = list(state_shapes.values()) + list(gradient_shapes.values())
    shapes += group_buffers(sum(early_rows)) + group_buffers(sum(late_rows))
    vmem = pl.BlockSpec(memory_space=pltpu.VMEM)
    d_alpha, losses, total = pl.pallas_call(
        functools.partial(kernel, names, frames_total),
        out_shape=[
            jax.ShapeDtypeStruct((images, side), f32),
            jax.ShapeDtypeStruct((1, side), f32),
            jax.ShapeDtypeStruct((896, 2 * side), f32),
        ],
        in_specs=[pl.BlockSpec(memory_space=pltpu.HBM)] * len(operands),
        out_specs=[vmem] * 3,
        scratch_shapes=[pltpu.VMEM(shape, f32) for shape in shapes]
        + [pltpu.SemaphoreType.DMA((len(operands),))]
        + [pltpu.SemaphoreType.DMA((2, 64))] * 3,
        compiler_params=pltpu.CompilerParams(
            collective_id=0, has_side_effects=True, vmem_limit_bytes=63 << 20
        ),
    )(
        recorded_exposures.reshape(images, side, side),
        embed, first, second, head.T, transform_tables(), screens,
    )
    start = lax.axis_index("dp") * regions
    return (
        d_alpha[:, :modes].reshape(regions, -1, modes),
        total[:256],
        total[256:512],
        total[512:768],
        total[768 : 768 + modes].T,
        lax.dynamic_slice(losses, (0, start), (1, regions))[0],
    )


def solution(mesh):
    return jax.shard_map(
        local,
        mesh=mesh,
        in_specs=(P("dp", "frame", None, None), P(), P(), P(), P(), P()),
        out_specs=(P("dp", "frame", None), P(), P(), P(), P(), P("dp")),
        check_vma=False,
    )
```

time: 82.8 us -> 71.1 us (0.86)
  Pallas kernels: 76 us -> 64.4 us
  other arithmetic: 1.26 us -> 0 us
  local copies, waits for them, and re-layouts: 4.69 us -> 5.9 us
    pallas_call x1, Pallas kernels: 76 us -> 64.4 us  [local(): pl.pallas_call(functools.partial(kernel, names, frames_total), out_shape=...]
    div x1 -> x0, other arithmetic: 1.26 us -> none  [local(): losses / (group * frames_here)]
    squeeze x0 -> x1, local copies, waits for them, and re-layouts: none -> 1.22 us  [local(): lax.dynamic_slice(losses, (0, start), (1, regions))[0]]
where the time goes in v2:
time: 71.1 us; the launch traced here: 70.9 us
  Pallas kernels  64.4 us (91%)
  local copies, waits for them, and re-layouts  5.9 us (8%)
    pallas_call x1, Pallas kernels, local(): pl.pallas_call(functools.partial(kernel, names, frames_total), out_shape=...  64.4 us
    slice x1, local copies, waits for them, and re-layouts, local(): total[512:768]  2 us

profile of v2, /device:TPU:1, one launch (start us, length us, event | category | flops | bytes accessed | tf_op | source)
XLA Modules:
  0.0 70.9 jit_solution(8857307077780261248)
XLA Ops:
  0.6 64.4 %shard_map.118 = (f32[8,128]{1,0:T(8,128)}, f32[1,128]{1,0:T(1,128)}, f32[896,256]{1,0:T(8,128)}) custom-call(f32[8,128,128]{2,1,0:T(8,128)} %bitcast.8, f32[256,256]{1,0:T(8,128)} %refs_1_.1, f32[256,256]{1,0:T(8,128)} %refs_2_.1, f32[256,256]{1,0:T(8,128)} %refs_3_.1, f32[44,256]{1,0:T(8,128)} %bitcast.9, f32[1680,256]{1,0:T(8,128)} %constant.14.clone.refs_5_, ...), custom_call_target="tpu_custom_call" | custom-call | tf_op jit(solution)/shard_map/pallas_call | solution.py:646
  65.0 1.2 %dynamic-slice_bitcast_fusion = f32[2]{0:T(128)} fusion(f32[1,128]{1,0:T(1,128)} %get-tuple-element.11, s32[]{:T(128)S(6)} %select_n.3), kind=kLoop, calls=%fused_computation.1 | loop fusion | bytes 20 | tf_op jit(solution)/shard_map/squeeze | solution.py:672
  66.2 1.4 %slice_bitcast_fusion = f32[256,44]{0,1:T(8,128)} fusion(f32[896,256]{1,0:T(8,128)} %get-tuple-element.10), kind=kLoop, calls=%fused_computation | loop fusion | bytes 90112 | tf_op jit(solution)/shard_map/transpose | solution.py:671
  67.7 2.0 %fusion = (f32[256,256]{1,0:T(8,128)}, f32[256,256]{1,0:T(8,128)}, f32[256,256]{1,0:T(8,128)}) fusion(f32[896,256]{1,0:T(8,128)} %get-tuple-element.10), kind=kLoop, calls=%fused_computation.2 | loop fusion | bytes 1572864 | tf_op jit(solution)/shard_map/slice | solution.py:670
  69.7 1.3 %copy.14 = f32[2,4,44]{2,1,0:T(4,128)} copy(f32[2,4,44]{2,1,0:T(4,128)} %bitcast.10) | data formatting | bytes 2816

commit v3 on v2

--- a/solution.py
+++ b/solution.py
@@ -635,6 +635,33 @@
     loss_ref[...] = total_ref[at : at + 1, 0:side] * (1.0 / frames_total)
 
 
+def hand_out(
+    alpha_ref, loss_ref, total_ref, embed_ref, first_ref, second_ref, head_ref, out_alpha_ref,
+    out_loss_ref, head, alpha, loss, sems,
+):
+    outs = (embed_ref, first_ref, second_ref)
+    copies = [
+        pltpu.make_async_copy(total_ref.at[256 * i : 256 * (i + 1)], out, sems.at[i])
+        for i, out in enumerate(outs)
+    ]
+    for copy in copies:
+        copy.start()
+    head[...] = total_ref[768 : 768 + modes, :]
+    regions = alpha.shape[0]
+    lane = lax.broadcasted_iota(jnp.int32, (1, side), 1)
+    at = lax.axis_index("dp") * regions
+    for p in range(regions):
+        alpha[p] = alpha_ref[p * frames_here : (p + 1) * frames_here, 0:modes]
+        one = jnp.where(lane == at + p, loss_ref[...], 0.0)
+        loss[:, p : p + 1] = jnp.sum(one, axis=1, keepdims=True)
+    small = ((head, head_ref), (alpha, out_alpha_ref), (loss, out_loss_ref))
+    for i, (src, dst) in enumerate(small):
+        copies.append(pltpu.make_async_copy(src, dst, sems.at[3 + i]))
+        copies[-1].start()
+    for copy in copies:
+        copy.wait()
+
+
 def local(recorded_exposures, screens, embed, first, second, head):
     regions = recorded_exposures.shape[0]
     frames_total = recorded_exposures.shape[1] * lax.axis_size("frame")
@@ -656,21 +683,35 @@
         + [pltpu.SemaphoreType.DMA((len(operands),))]
         + [pltpu.SemaphoreType.DMA((2, 64))] * 3,
         compiler_params=pltpu.CompilerParams(
-            collective_id=0, has_side_effects=True, vmem_limit_bytes=63 << 20
+            collective_id=0, has_side_effects=True, vmem_limit_bytes=40 << 20
         ),
     )(
-        recorded_exposures.reshape(images, side, side),
-        embed, first, second, head.T, transform_tables(), screens,
+        *(
+            pltpu.with_memory_space_constraint(operand, pltpu.HBM)
+            for operand in (
+                recorded_exposures.reshape(images, side, side),
+                embed, first, second, head.T, jnp.asarray(transform_tables()), screens,
+            )
+        )
     )
-    start = lax.axis_index("dp") * regions
-    return (
-        d_alpha[:, :modes].reshape(regions, -1, modes),
-        total[:256],
-        total[256:512],
-        total[512:768],
-        total[768 : 768 + modes].T,
-        lax.dynamic_slice(losses, (0, start), (1, regions))[0],
-    )
+    out = pl.pallas_call(
+        hand_out,
+        out_shape=[jax.ShapeDtypeStruct((256, 256), f32)] * 3
+        + [
+            jax.ShapeDtypeStruct((modes, 256), f32),
+            jax.ShapeDtypeStruct((regions, frames_here, modes), f32),
+            jax.ShapeDtypeStruct((1, regions), f32),
+        ],
+        in_specs=[vmem] * 3,
+        out_specs=[pl.BlockSpec(memory_space=pltpu.HBM)] * 6,
+        scratch_shapes=[
+            pltpu.VMEM((modes, 256), f32),
+            pltpu.VMEM((regions, frames_here, modes), f32),
+            pltpu.VMEM((1, regions), f32),
+            pltpu.SemaphoreType.DMA((6,)),
+        ],
+    )(d_alpha, losses, total)
+    return (out[4], out[0], out[1], out[2], out[3].T, out[5].reshape(regions))
 
 
 def solution(mesh):

time: 71.1 us -> 68.3 us (0.961)
  local copies, waits for them, and re-layouts: 5.9 us -> 2.02 us
  Pallas kernels: 64.4 us -> 65.6 us
    pallas_call x0 -> x1, Pallas kernels: none -> 2.12 us  [local(): pl.pallas_call(hand_out, out_shape=[jax.ShapeDtypeStruct((256, 256), f32)...]
    slice x1 -> x0, local copies, waits for them, and re-layouts: 2 us -> none  [local(): total[512:768]]
    transpose x1 -> x0, local copies, waits for them, and re-layouts: 1.42 us -> none  [local(): total[768:768 + modes]]
    squeeze x1 -> x0, local copies, waits for them, and re-layouts: 1.22 us -> none  [local(): lax.dynamic_slice(losses, (0, start), (1, regions))[0]]
    pallas_call x1, Pallas kernels: 64.4 us -> 63.5 us  [local(): pl.pallas_call(functools.partial(kernel, names, frames_total), out_shape=...]
    unnamed x1 -> x6, local copies, waits for them, and re-layouts: 1.27 us -> 2.02 us
where the time goes in v3:
time: 68.3 us; the launch traced here: 68.2 us
  Pallas kernels  65.6 us (96%)
  local copies, waits for them, and re-layouts  2.02 us (3%)
    pallas_call x1, Pallas kernels, local(): pl.pallas_call(functools.partial(kernel, names, frames_total), out_shape=...  63.5 us
    pallas_call x1, Pallas kernels, local(): pl.pallas_call(hand_out, out_shape=[jax.ShapeDtypeStruct((256, 256), f32)...  2.12 us
    unnamed x6, local copies, waits for them, and re-layouts  2.02 us

profile of v3, /device:TPU:1, one launch (start us, length us, event | category | flops | bytes accessed | tf_op | source)
XLA Modules:
  0.0 68.2 jit_solution(7376986410238761745)
XLA Ops:
  0.6 63.5 %shard_map.118 = (f32[8,128]{1,0:T(8,128)S(1)}, f32[1,128]{1,0:T(1,128)S(1)}, f32[896,256]{1,0:T(8,128)S(1)}) custom-call(f32[8,128,128]{2,1,0:T(8,128)} %bitcast.4, f32[256,256]{1,0:T(8,128)} %refs_1_.1, f32[256,256]{1,0:T(8,128)} %refs_2_.1, f32[256,256]{1,0:T(8,128)} %refs_3_.1, f32[44,256]{1,0:T(8,128)} %bitcast.5, f32[1680,256]{1,0:T(8,128)} %constant.2.clone.refs_5_, ...), custom_call_target="tpu_custom_call" | custom-call | tf_op jit(solution)/shard_map/pallas_call | solution.py:673
  64.1 0.0 copy-start
  64.1 0.9 %copy-done = f32[896,256]{1,0:T(8,128)} copy-done((f32[896,256]{1,0:T(8,128)}, f32[896,256]{1,0:T(8,128)S(1)}, u32[]{:S(2)}) %copy-start) | copy-done | bytes 917528
  65.0 0.0 copy-start.1
  65.0 0.6 copy-done.1
  65.6 0.0 copy-start.2
  65.6 0.5 copy-done.2
  66.1 2.1 %shard_map.119 = (f32[256,256]{1,0:T(8,128)}, f32[256,256]{1,0:T(8,128)}, f32[256,256]{1,0:T(8,128)}, f32[44,256]{1,0:T(8,128)}, f32[2,4,44]{2,1,0:T(4,128)}, /*index=5*/f32[1,2]{1,0:T(1,128)}) custom-call(f32[8,128]{1,0:T(8,128)} %copy-done.1, f32[1,128]{1,0:T(1,128)} %copy-done.2, f32[896,256]{1,0:T(8,128)} %copy-done), custom_call_target="tpu_custom_call" | custom-call | tf_op jit(solution)/shard_map/pallas_call | solution.py:697
Async XLA Ops:
  64.1 0.9 %copy-start = (f32[896,256]{1,0:T(8,128)}, f32[896,256]{1,0:T(8,128)S(1)}, u32[]{:S(2)}) copy-start(f32[896,256]{1,0:T(8,128)S(1)} %get-tuple-element.17.total_ref) | copy-start | bytes 2752516
  65.0 0.6 copy-start.1
  65.6 0.5 copy-start.2

commit v4 on v3

--- a/solution.py
+++ b/solution.py
@@ -1,4 +1,5 @@
 import functools
+import math
 import types
 
 import jax
@@ -105,8 +106,7 @@
 
 def cut_tiles(img, tiles):
     group = lax.broadcasted_iota(jnp.int32, (8, side), 1) // 16
-
-    def one(n, carry):
+    for n in range(images):
         for g in range(2):
             x = [img[n, pl.ds(8 * g + j, 8, stride=16), :] for j in range(8)]
             for bit in (1, 2, 4):
@@ -119,10 +119,8 @@
                         y[q] = jnp.where(low, pltpu.roll(x[p], side - 16 * bit, 1), x[q])
                 x = y
             for c in range(8):
-                tiles[pl.ds(pl.multiple_of(n * 64 + c * 8, 8), 8), g * side : (g + 1) * side] = x[c]
-        return carry
-
-    lax.fori_loop(0, images, one, 0)
+                row = n * tiles_each + c * 8
+                tiles[row : row + 8, g * side : (g + 1) * side] = x[c]
 
 
 def tile_sum(value):
@@ -146,11 +144,42 @@
     return dot_nt(mean, s.head[...], HIGHEST)
 
 
+def chop(value, bits):
+    mantissa, exponent = math.frexp(value)
+    return math.ldexp(math.floor(mantissa * 2**bits), exponent - bits)
+
+
+def pieces(value, bits, number):
+    out = []
+    for _ in range(number - 1):
+        out.append(chop(value, bits))
+        value -= out[-1]
+    return out + [value]
+
+
+def cos_sin(x):
+    turns = jnp.round(x * (1.0 / (512.0 * math.pi)))
+    for piece in pieces(512.0 * math.pi, 8, 4):
+        x = x - turns * piece
+    quarter = jnp.round(x * (2.0 / math.pi))
+    for piece in pieces(0.5 * math.pi, 12, 3):
+        x = x - quarter * piece
+    z = x * x
+    sin = x + x * z * (-1.6666654611e-1 + z * (8.3321608736e-3 + z * -1.9515295891e-4))
+    cos = 1.0 - 0.5 * z + z * z * (4.166664568298827e-2 + z * (-1.388731625493765e-3 + z * 2.443315711809948e-5))
+    quadrant = quarter.astype(jnp.int32)
+    odd = (quadrant & 1) != 0
+    cos, sin = jnp.where(odd, sin, cos), jnp.where(odd, cos, sin)
+    cos = jnp.where(((quadrant + 1) & 2) != 0, -cos, cos)
+    sin = jnp.where((quadrant & 2) != 0, -sin, sin)
+    return cos, sin
+
+
 def pupil_field(alpha, screens, spread, field):
     for m in range(modes):
         spread[m] = jnp.broadcast_to(alpha[:, m : m + 1], (images, side))
     lane = lax.broadcasted_iota(jnp.int32, (images, side), 1) - half
-    width = 5
+    width = 13
 
     def rows(block, carry):
         at = [pl.multiple_of((block * width + i) * side, side) for i in range(width)]
@@ -162,13 +191,14 @@
         for i in range(width):
             up = block * width + i - half // 2
             inside = lane * lane + up * up <= (side // 4) ** 2
-            field[block * width + i, :, 0:side] = jnp.where(inside, jnp.cos(total[i]), 0.0)
-            field[block * width + i, :, side : 2 * side] = jnp.where(inside, jnp.sin(total[i]), 0.0)
+            cos, sin = cos_sin(total[i])
+            at = pl.ds(pl.multiple_of((block * width + i) * images, images), images)
+            field[at, 0:side] = jnp.where(inside, cos, 0.0)
+            field[at, side : 2 * side] = jnp.where(inside, sin, 0.0)
         return carry
 
     lax.fori_loop(0, span // width, rows, 0)
-    for i in range(span, pad_span):
-        field[i] = jnp.zeros((images, 2 * side), jnp.float32)
+    field[span * images :, :] = jnp.zeros(((pad_span - span) * images, 2 * side), jnp.float32)
 
 
 def patch_lanes(p):
@@ -202,13 +232,17 @@
         s.spec[n, 0:8, :] = jnp.where(edge_slot(2 * side), value, s.spec[n, 0:8, :])
 
 
-def frame_energy(s):
+def prepare_backward(s):
     for n in range(images):
         s.energy[n : n + 1, :] = jnp.sum(s.img[n] * s.img[n], axis=0, keepdims=True)
+    s.tiles_t[...] = s.tiles[...].T
+    s.hidden_t[...] = silu_act(s.hid_pre[...]).T
+    s.hid_pre[...] = silu_slope(s.hid_pre[...])
+    s.inn_pre[...] = silu_slope(s.inn_pre[...])
 
 
 def pupil_rows(s, t):
-    rowed = dot(s.field[...].reshape(pad_span * images, 2 * side), t.both[...])
+    rowed = dot(s.field[...], t.both[...])
     s.rowed_r[...] = rowed[:, 0:side]
     s.rowed_i[...] = rowed[:, side : 2 * side]
     for n in range(images):
@@ -277,37 +311,18 @@
 
 
 def alpha_adjoint(s, t):
-    screens = s.screens
     for n in range(images):
         lanes = slice(n * side, (n + 1) * side)
         rows = pl.ds(n, pad_span, stride=images)
         s.rowed_r[rows, :] = s.stack[0:pad_span, lanes]
         s.rowed_i[rows, :] = s.stack[pad_span : 2 * pad_span, lanes]
     rowed = jnp.concatenate([s.rowed_r[...], s.rowed_i[...]], axis=1)
-    d_field = dot(rowed, t.both_t[...]).reshape(pad_span, images, 2 * side)
-    f_r, f_i = s.field[:, :, 0:side], s.field[:, :, side : 2 * side]
-    s.phase[...] = d_field[:, :, side : 2 * side] * f_r - d_field[:, :, 0:side] * f_i
-
-    alpha_lane = lax.broadcasted_iota(jnp.int32, (images, side), 1)
-    d_alpha = jnp.zeros((images, side), jnp.float32)
-    chunk = 11
-    for start in range(0, modes, chunk):
-
-        def rows(i, total, start=start):
-            value = s.phase[i]
-            at = pl.multiple_of(i * side, side)
-            return tuple(
-                total[m] + value * screens[start + m : start + m + 1, pl.ds(at, side)]
-                for m in range(chunk)
-            )
-
-        zero = tuple(jnp.zeros((images, side), jnp.float32) for _ in range(chunk))
-        total = lax.fori_loop(0, span, rows, zero)
-        for m in range(chunk):
-            d_alpha = jnp.where(
-                alpha_lane == start + m, jnp.sum(total[m], axis=1, keepdims=True), d_alpha
-            )
-    return d_alpha
+    d_field = dot(rowed, t.both_t[...])
+    f_r, f_i = s.field[:, 0:side], s.field[:, side : 2 * side]
+    phase = d_field[:, side : 2 * side] * f_r - d_field[:, 0:side] * f_i
+
+    phase = jnp.concatenate([phase[i * images : (i + 1) * images] for i in range(span)], axis=1)
+    return dot_nt(s.screens[...], phase)
 
 
 def spread(value):
@@ -315,32 +330,34 @@
 
 
 def gradients_after_mean(s, d_alpha):
-    s.grad_tail[...] = dot_tn(d_alpha, s.pooled[...])
-    d_pooled = dot(d_alpha[:, 0:modes], s.head[...]) * (1.0 / tiles_each)
+    s.grad_tail[0:modes, :] = dot(d_alpha, s.pooled[...])
+    d_pooled = dot_tn(d_alpha, s.head[...]) * (1.0 / tiles_each)
     s.grad_second[...] = dot_tn(s.inner_sum[...], d_pooled)
     return d_pooled
 
 
 def gradient_first(s, d_pooled):
-    d_inner = spread(dot_nt(d_pooled, s.second[...])) * silu_slope(s.inn_pre[...])
-    s.grad_first[...] = dot_tn(silu_act(s.hid_pre[...]), d_inner)
+    d_inner = spread(dot_nt(d_pooled, s.second[...])) * s.inn_pre[...]
+    s.grad_first[...] = dot(s.hidden_t[...], d_inner)
     return d_inner
 
 
 def gradient_embed(s, d_pooled, d_inner):
     d_hidden = spread(d_pooled) + dot_nt(d_inner, s.first[...])
-    s.grad_embed[...] = dot_tn(s.tiles[...], d_hidden * silu_slope(s.hid_pre[...]))
+    s.grad_embed[...] = dot(s.tiles_t[...], d_hidden * s.hid_pre[...])
 
 
 state_shapes = dict(
     tiles=(images * tiles_each, 256),
     hid_pre=(images * tiles_each, 256),
     inn_pre=(images * tiles_each, 256),
+    tiles_t=(256, images * tiles_each),
+    hidden_t=(256, images * tiles_each),
     inner_sum=(images, 256),
     pooled=(images, 256),
     energy=(images, side),
     spread=(modes, images, side),
-    field=(pad_span, images, 2 * side),
+    field=(pad_span * images, 2 * side),
     rowed_r=(pad_span * images, side),
     rowed_i=(pad_span * images, side),
     stack=(2 * pad_span, images * side),
@@ -353,7 +370,6 @@
     merged=(16, 16, side),
     inbox=(15, 16, side),
     ratio=(32, 8, side),
-    phase=(pad_span, images, side),
     screens=(modes, span * side),
     img=(images, side, side),
     embed=(256, 256),
@@ -449,7 +465,7 @@
             copy.wait_send()
 
 
-def spectral_exchange(s, regularizer_strength, sems):
+def spectral_exchange(s, regularizer_strength, sems, meanwhile):
     place, mail = Place(), Mail(sems)
     core, seat = place.core, place.seat
     swap = mail.send(s.part.at[pl.ds((1 - core) * 16, 16)], s.core_part, place.sibling())
@@ -459,6 +475,7 @@
     for i, step in reversed(list(enumerate(burst_steps))):
         there, device = place.burst(step)
         copies[i] = mail.send(s.merged.at[there], s.inbox.at[i], device)
+    meanwhile()
     total = s.merged[seat]
     for i in range(len(burst_steps)):
         copies[i].wait_recv()
@@ -599,12 +616,14 @@
     for p in patches:
         frame_spectra(s, t, p)
         spectral_sums(s, t, p)
-    frame_energy(s)
     pl.semaphore_wait(pltpu.get_barrier_semaphore(), greeted)
-    spectral_exchange(s, regularizer_relative * frames_total, spectral_sems)
+    spectral_exchange(
+        s, regularizer_relative * frames_total, spectral_sems, lambda: prepare_backward(s)
+    )
     losses = [focal_adjoint(s, t, p) for p in patches]
     d_alpha = alpha_adjoint(s, t)
-    alpha_ref[...] = d_alpha
+    alpha_ref[:, 0:modes] = d_alpha.T
+    s.grad_tail[modes:, :] = jnp.zeros((side - modes, 2 * side), jnp.float32)
 
     early = GradientGroup(((s.grad_second, 0), (s.grad_tail, 256)), buffers[:6], early_sems)
     late = GradientGroup(((s.grad_first, 0), (s.grad_embed, 256)), buffers[6:], late_sems)
@@ -710,6 +729,7 @@
             pltpu.VMEM((1, regions), f32),
             pltpu.SemaphoreType.DMA((6,)),
         ],
+        compiler_params=pltpu.CompilerParams(vmem_limit_bytes=2 << 20),
     )(d_alpha, losses, total)
     return (out[4], out[0], out[1], out[2], out[3].T, out[5].reshape(regions))
 

time: 68.3 us -> 62.7 us (0.918)
  Pallas kernels: 65.6 us -> 61.8 us
  local copies, waits for them, and re-layouts: 2.02 us -> 0 us
    pallas_call x1, Pallas kernels: 63.5 us -> 60.9 us  [local(): pl.pallas_call(functools.partial(kernel, names, frames_total), out_shape=...]
    unnamed x6 -> x0, local copies, waits for them, and re-layouts: 2.02 us -> none
    pallas_call x1, Pallas kernels: 2.12 us -> 0.94 us  [local(): pl.pallas_call(hand_out, out_shape=[jax.ShapeDtypeStruct((256, 256), f32)...]
where the time goes in v4:
time: 62.7 us; the launch traced here: 62.6 us
  Pallas kernels  61.8 us (99%)
  between operations  0.8 us (1%)
    pallas_call x1, Pallas kernels, local(): pl.pallas_call(functools.partial(kernel, names, frames_total), out_shape=...  60.9 us

profile of v4, /device:TPU:1, one launch (start us, length us, event | category | flops | bytes accessed | tf_op | source)
XLA Modules:
  0.0 62.6 jit_solution(9712663607105573514)
XLA Ops:
  0.6 60.9 %shard_map.118 = (f32[8,128]{1,0:T(8,128)S(1)}, f32[1,128]{1,0:T(1,128)S(1)}, f32[896,256]{1,0:T(8,128)S(1)}) custom-call(f32[8,128,128]{2,1,0:T(8,128)} %bitcast.4, f32[256,256]{1,0:T(8,128)} %refs_1_.1, f32[256,256]{1,0:T(8,128)} %refs_2_.1, f32[256,256]{1,0:T(8,128)} %refs_3_.1, f32[44,256]{1,0:T(8,128)} %bitcast.5, f32[1680,256]{1,0:T(8,128)} %constant.2.clone.refs_5_, ...), custom_call_target="tpu_custom_call" | custom-call | tf_op jit(solution)/shard_map/pallas_call | solution.py:692
  61.5 0.9 %shard_map.119 = (f32[256,256]{1,0:T(8,128)}, f32[256,256]{1,0:T(8,128)}, f32[256,256]{1,0:T(8,128)}, f32[44,256]{1,0:T(8,128)}, f32[2,4,44]{2,1,0:T(4,128)}, /*index=5*/f32[1,2]{1,0:T(1,128)}) custom-call(f32[8,128]{1,0:T(8,128)S(1)} %get-tuple-element.15.alpha_ref, f32[1,128]{1,0:T(1,128)S(1)} %get-tuple-element.16.loss_ref, ...), custom_call_target="tpu_custom_call" | custom-call | tf_op jit(solution)/shard_map/pallas_call | solution.py:716

commit v5 on v4

--- a/solution.py
+++ b/solution.py
@@ -24,6 +24,7 @@
 modes = 44
 tiles_each = 64
 loss_row = 44
+second_row = 48
 
 
 def dot(a, b, precision=HIGH):
@@ -202,15 +203,25 @@
 
 
 def patch_lanes(p):
-    return slice(p * frames_here * side, (p + 1) * frames_here * side)
+    width = frames_here * side
+    return pl.ds(pl.multiple_of(p * width, width), width)
+
+
+def frame_lanes(n):
+    return pl.ds(pl.multiple_of(n * side, side), side)
+
+
+def patch_rows(p):
+    return pl.ds(p * 16, 16)
 
 
 def real_transform(planes, first_table, second_table, s, p, out):
     lanes = patch_lanes(p)
     s.staged[:, lanes] = dot(first_table[...], planes)
     edge = []
-    for n in range(p * frames_here, (p + 1) * frames_here):
-        lanes = slice(n * side, (n + 1) * side)
+    for f in range(frames_here):
+        n = p * frames_here + f
+        lanes = frame_lanes(n)
         edge.append(jnp.sum(s.staged[0:1, lanes] * alternating(1), axis=1, keepdims=True))
         pair = jnp.concatenate([s.staged[0:side, lanes], s.staged[side : 2 * side, lanes]], axis=1)
         out[n] = dot(pair, second_table[...])
@@ -224,17 +235,18 @@
 
 
 def frame_spectra(s, t, p):
-    here = range(p * frames_here, (p + 1) * frames_here)
+    here = [p * frames_here + f for f in range(frames_here)]
     planes = jnp.concatenate([s.img[n] for n in here], axis=1)
     edge = real_transform(planes, t.real, t.swapped, s, p, s.spec)
-    for n in here:
-        value = edge[n - here[0]] * (1.0 / side)
+    for f, n in enumerate(here):
+        value = edge[f] * (1.0 / side)
         s.spec[n, 0:8, :] = jnp.where(edge_slot(2 * side), value, s.spec[n, 0:8, :])
 
 
 def prepare_backward(s):
     for n in range(images):
-        s.energy[n : n + 1, :] = jnp.sum(s.img[n] * s.img[n], axis=0, keepdims=True)
+        at = n % frames_here
+        s.energy[n // frames_here, at : at + 1, :] = jnp.sum(s.img[n] * s.img[n], axis=0, keepdims=True)
     s.tiles_t[...] = s.tiles[...].T
     s.hidden_t[...] = silu_act(s.hid_pre[...]).T
     s.hid_pre[...] = silu_slope(s.hid_pre[...])
@@ -270,8 +282,8 @@
     num = jnp.where(real_slot, t1 + pltpu.roll(t1, half, 1), turned - t2)
     num = jnp.where(at_corner, t1, num)
     den = jnp.where(at_corner, t3, t3 + pltpu.roll(t3, half, 1))
-    s.part[p * 16 : (p + 1) * 16, 0:8, :] = num.reshape(16, 8, side)
-    s.part[p * 16 : (p + 1) * 16, 8:16, :] = den.reshape(16, 8, side)
+    s.part[patch_rows(p), 0:8, :] = num.reshape(16, 8, side)
+    s.part[patch_rows(p), 8:16, :] = den.reshape(16, 8, side)
 
 
 def total_of(value):
@@ -283,19 +295,19 @@
     real_slot, at_corner = lane < half, corner(side)
     per_pixel = 1.0 / (side * side)
     weight = jnp.where(lax.rem(lane, half) == 0, per_pixel, 2.0 * per_pixel)
-    rho = s.ratio[p * 16 : (p + 1) * 16].reshape(side, side)
-    num = s.part[p * 16 : (p + 1) * 16, 0:8, :].reshape(side, side)
+    rho = s.ratio[patch_rows(p)].reshape(side, side)
+    num = s.part[patch_rows(p), 0:8, :].reshape(side, side)
     turned = pltpu.roll(rho, half, 1)
     square = rho * rho
     a = jnp.where(jnp.logical_or(real_slot, at_corner), rho, turned) * (-2.0 * weight)
     b = jnp.where(real_slot, turned, -rho)
     b = jnp.where(at_corner, 0.0, b) * (-2.0 * weight)
     m = jnp.where(at_corner, square, square + turned * turned) * (2.0 * weight)
-    energy = total_of(s.energy[p * frames_here : (p + 1) * frames_here, :])
+    energy = total_of(s.energy[p])
     loss = energy * per_pixel - total_of(weight * rho * num)
     for f in range(frames_here):
         n = p * frames_here + f
-        lanes = slice(n * side, (n + 1) * side)
+        lanes = frame_lanes(n)
         g = a * s.spec[n, :, 0:side] + b * s.spec[n, :, side : 2 * side] + m * s.otf[n]
         y = dot(g, t.half_plane_t[...])
         s.staged[0:side, lanes] = y[:, 0:side]
@@ -331,9 +343,13 @@
 
 def gradients_after_mean(s, d_alpha):
     s.grad_tail[0:modes, :] = dot(d_alpha, s.pooled[...])
-    d_pooled = dot_tn(d_alpha, s.head[...]) * (1.0 / tiles_each)
-    s.grad_second[...] = dot_tn(s.inner_sum[...], d_pooled)
-    return d_pooled
+    s.grad_tail[second_row : second_row + modes, :] = dot(d_alpha, s.inner_sum[...])
+    return dot_tn(d_alpha, s.head[...]) * (1.0 / tiles_each)
+
+
+def gradient_second(s, tail):
+    factor = tail[second_row : second_row + modes, :]
+    return dot_tn(factor, s.head[...], HIGHEST) * (1.0 / tiles_each)
 
 
 def gradient_first(s, d_pooled):
@@ -355,7 +371,7 @@
     hidden_t=(256, images * tiles_each),
     inner_sum=(images, 256),
     pooled=(images, 256),
-    energy=(images, side),
+    energy=(images // frames_here, frames_here, side),
     spread=(modes, images, side),
     field=(pad_span * images, 2 * side),
     rowed_r=(pad_span * images, side),
@@ -379,7 +395,7 @@
     tables=(1680, 256),
 )
 gradient_shapes = dict(
-    grad_embed=(256, 256), grad_first=(256, 256), grad_second=(256, 256), grad_tail=(128, 256)
+    grad_embed=(256, 256), grad_first=(256, 256), grad_tail=(128, 256), tail=(128, 256)
 )
 
 
@@ -465,34 +481,49 @@
             copy.wait_send()
 
 
-def spectral_exchange(s, regularizer_strength, sems, meanwhile):
-    place, mail = Place(), Mail(sems)
-    core, seat = place.core, place.seat
-    swap = mail.send(s.part.at[pl.ds((1 - core) * 16, 16)], s.core_part, place.sibling())
-    swap.wait_recv()
-    s.merged[...] = s.part[pl.ds(core * 16, 16)] + s.core_part[...]
-    copies = {}
-    for i, step in reversed(list(enumerate(burst_steps))):
-        there, device = place.burst(step)
-        copies[i] = mail.send(s.merged.at[there], s.inbox.at[i], device)
-    meanwhile()
-    total = s.merged[seat]
-    for i in range(len(burst_steps)):
-        copies[i].wait_recv()
-        total = total + s.inbox[i]
-    mine = core * 16 + seat
-    s.ratio[mine] = total[0:8] / (total[8:16] + regularizer_strength)
-    copies = {}
-    for i, step in reversed(list(enumerate(burst_steps))):
-        copies[i] = mail.send(s.ratio.at[mine], s.ratio.at[mine], place.burst(step)[1])
-    passed = [mail.send(s.ratio.at[mine], s.ratio.at[mine], place.sibling())]
-    for i, step in enumerate(burst_steps):
-        copies[i].wait_recv()
-        came = core * 16 + place.burst(step, -1)[0]
-        passed.append(mail.send(s.ratio.at[came], s.ratio.at[came], place.sibling()))
-    for copy in passed:
-        copy.wait_recv()
-    mail.finish()
+class SpectralExchange:
+    def __init__(self, s, sems):
+        self.s, self.place, self.mail = s, Place(), Mail(sems)
+        self.core, self.seat = self.place.core, self.place.seat
+
+    def send_core(self):
+        theirs = pl.ds((1 - self.core) * 16, 16)
+        self.swap = self.mail.send(self.s.part.at[theirs], self.s.core_part, self.place.sibling())
+
+    def send_burst(self):
+        s = self.s
+        self.swap.wait_recv()
+        s.merged[...] = s.part[pl.ds(self.core * 16, 16)] + s.core_part[...]
+        self.copies = {}
+        for i, step in reversed(list(enumerate(burst_steps))):
+            there, device = self.place.burst(step)
+            self.copies[i] = self.mail.send(s.merged.at[there], s.inbox.at[i], device)
+
+    def send_back(self, regularizer_strength):
+        s = self.s
+        total = s.merged[self.seat]
+        for i in range(len(burst_steps)):
+            self.copies[i].wait_recv()
+            total = total + s.inbox[i]
+        mine = self.core * 16 + self.seat
+        s.ratio[mine] = total[0:8] / (total[8:16] + regularizer_strength)
+        self.copies = {}
+        for i, step in reversed(list(enumerate(burst_steps))):
+            device = self.place.burst(step)[1]
+            self.copies[i] = self.mail.send(s.ratio.at[mine], s.ratio.at[mine], device)
+        self.passed = [self.mail.send(s.ratio.at[mine], s.ratio.at[mine], self.place.sibling())]
+
+    def pass_on(self):
+        ratio = self.s.ratio
+        for i, step in enumerate(burst_steps):
+            self.copies[i].wait_recv()
+            came = self.core * 16 + self.place.burst(step, -1)[0]
+            self.passed.append(self.mail.send(ratio.at[came], ratio.at[came], self.place.sibling()))
+
+    def finish(self):
+        for copy in self.passed:
+            copy.wait_recv()
+        self.mail.finish()
 
 
 class GradientGroup:
@@ -585,8 +616,8 @@
 
 
 operands = ("img", "embed", "first", "second", "head", "tables", "screens")
-early_rows = (256, 128)
-late_rows = (256, 256)
+early_rows = (128, 256)
+late_rows = (256,)
 
 
 def kernel(names, frames_total, *refs):
@@ -612,46 +643,51 @@
     pupil_field(alpha, s.screens, s.spread, s.field)
     s.wait("tables")
     pupil_rows(s, t)
-    patches = range(images // frames_here)
-    for p in patches:
-        frame_spectra(s, t, p)
-        spectral_sums(s, t, p)
+    mine = lax.rem(lax.axis_index("frame"), 2)
+    burst = SpectralExchange(s, spectral_sems)
+    frame_spectra(s, t, 1 - mine)
+    spectral_sums(s, t, 1 - mine)
     pl.semaphore_wait(pltpu.get_barrier_semaphore(), greeted)
-    spectral_exchange(
-        s, regularizer_relative * frames_total, spectral_sems, lambda: prepare_backward(s)
-    )
-    losses = [focal_adjoint(s, t, p) for p in patches]
+    burst.send_core()
+    frame_spectra(s, t, mine)
+    spectral_sums(s, t, mine)
+    burst.send_burst()
+    prepare_backward(s)
+    burst.send_back(regularizer_relative * frames_total)
+    burst.pass_on()
+    losses = [(mine, focal_adjoint(s, t, mine))]
+    burst.finish()
+    losses.append((1 - mine, focal_adjoint(s, t, 1 - mine)))
     d_alpha = alpha_adjoint(s, t)
     alpha_ref[:, 0:modes] = d_alpha.T
-    s.grad_tail[modes:, :] = jnp.zeros((side - modes, 2 * side), jnp.float32)
-
-    early = GradientGroup(((s.grad_second, 0), (s.grad_tail, 256)), buffers[:6], early_sems)
-    late = GradientGroup(((s.grad_first, 0), (s.grad_embed, 256)), buffers[6:], late_sems)
+
+    early = GradientGroup(((s.grad_tail, 0), (s.grad_first, 128)), buffers[:6], early_sems)
+    late = GradientGroup(((s.grad_embed, 0),), buffers[6:], late_sems)
+    s.grad_tail[...] = jnp.zeros_like(s.grad_tail)
     d_pooled = gradients_after_mean(s, d_alpha)
     lane = lax.broadcasted_iota(jnp.int32, (1, side), 1)
     row = jnp.zeros((1, side), jnp.float32)
-    for p in patches:
-        at = lax.axis_index("dp") * len(patches) + p
-        row = jnp.where(lane == at, losses[p], row)
+    for p, loss in losses:
+        row = jnp.where(lane == lax.axis_index("dp") * len(losses) + p, loss, row)
     s.grad_tail[loss_row : loss_row + 1, 0:side] = row
     early.send_core(0)
+    d_inner = gradient_first(s, d_pooled)
     early.send_core(1)
-    d_inner = gradient_first(s, d_pooled)
+    gradient_embed(s, d_pooled, d_inner)
     late.send_core(0)
     early.send_plane()
-    gradient_embed(s, d_pooled, d_inner)
-    late.send_core(1)
     late.send_plane()
     early.send_column()
     late.send_column()
     early.send_back()
     late.send_back()
     early.pass_on()
+    early.finish((s.tail, total_ref.at[256:512]))
+    total_ref[512:768, :] = gradient_second(s, s.tail)
+    total_ref[768 : 768 + modes, :] = s.tail[0:modes, :]
+    loss_ref[...] = s.tail[loss_row : loss_row + 1, 0:side] * (1.0 / frames_total)
     late.pass_on()
-    early.finish((total_ref.at[512:768], total_ref.at[768:896]))
-    late.finish((total_ref.at[256:512], total_ref.at[0:256]))
-    at = 768 + loss_row
-    loss_ref[...] = total_ref[at : at + 1, 0:side] * (1.0 / frames_total)
+    late.finish((total_ref.at[0:256],))
 
 
 def hand_out(
@@ -694,7 +730,7 @@
         out_shape=[
             jax.ShapeDtypeStruct((images, side), f32),
             jax.ShapeDtypeStruct((1, side), f32),
-            jax.ShapeDtypeStruct((896, 2 * side), f32),
+            jax.ShapeDtypeStruct((816, 2 * side), f32),
         ],
         in_specs=[pl.BlockSpec(memory_space=pltpu.HBM)] * len(operands),
         out_specs=[vmem] * 3,

time: 62.7 us -> 60.6 us (0.967)
  Pallas kernels: 61.8 us -> 59.7 us
    pallas_call x1, Pallas kernels: 60.9 us -> 58.8 us  [local(): pl.pallas_call(functools.partial(kernel, names, frames_total), out_shape=...]
where the time goes in v5:
time: 60.6 us; the launch traced here: 60.5 us
  Pallas kernels  59.7 us (99%)
  between operations  0.8 us (1%)
    pallas_call x1, Pallas kernels, local(): pl.pallas_call(functools.partial(kernel, names, frames_total), out_shape=...  58.8 us

profile of v5, /device:TPU:1, one launch (start us, length us, event | category | flops | bytes accessed | tf_op | source)
XLA Modules:
  0.0 60.5 jit_solution(5236449252206404436)
XLA Ops:
  0.6 58.8 %shard_map.118 = (f32[8,128]{1,0:T(8,128)S(1)}, f32[1,128]{1,0:T(1,128)S(1)}, f32[816,256]{1,0:T(8,128)S(1)}) custom-call(f32[8,128,128]{2,1,0:T(8,128)} %bitcast.4, f32[256,256]{1,0:T(8,128)} %refs_1_.1, f32[256,256]{1,0:T(8,128)} %refs_2_.1, f32[256,256]{1,0:T(8,128)} %refs_3_.1, f32[44,256]{1,0:T(8,128)} %bitcast.5, f32[1680,256]{1,0:T(8,128)} %constant.2.clone.refs_5_, ...), custom_call_target="tpu_custom_call" | custom-call | tf_op jit(solution)/shard_map/pallas_call | solution.py:728
  59.4 0.9 %shard_map.119 = (f32[256,256]{1,0:T(8,128)}, f32[256,256]{1,0:T(8,128)}, f32[256,256]{1,0:T(8,128)}, f32[44,256]{1,0:T(8,128)}, f32[2,4,44]{2,1,0:T(4,128)}, /*index=5*/f32[1,2]{1,0:T(1,128)}) custom-call(f32[8,128]{1,0:T(8,128)S(1)} %get-tuple-element.15.alpha_ref, f32[1,128]{1,0:T(1,128)S(1)} %get-tuple-element.16.loss_ref, ...), custom_call_target="tpu_custom_call" | custom-call | tf_op jit(solution)/shard_map/pallas_call | solution.py:752

commit v6 on v5

--- a/solution.py
+++ b/solution.py
@@ -129,19 +129,15 @@
 
 
 def encode(s):
-    s.wait("embed")
-    pre = dot(s.tiles[...], s.embed[...], HIGHEST)
+    pre = dot(s.tiles[...], s.embed[...])
     s.hid_pre[...] = pre
     hidden = silu_act(pre)
-    s.wait("first")
-    pre = dot(hidden, s.first[...], HIGHEST)
+    pre = dot(hidden, s.first[...])
     s.inn_pre[...] = pre
     total = tile_sum(silu_act(pre))
     s.inner_sum[...] = total
-    s.wait("second")
     mean = (tile_sum(hidden) + dot(total, s.second[...], HIGHEST)) * (1.0 / tiles_each)
     s.pooled[...] = mean
-    s.wait("head")
     return dot_nt(mean, s.head[...], HIGHEST)
 
 
@@ -247,6 +243,7 @@
     for n in range(images):
         at = n % frames_here
         s.energy[n // frames_here, at : at + 1, :] = jnp.sum(s.img[n] * s.img[n], axis=0, keepdims=True)
+    s.grad_tail[...] = jnp.zeros_like(s.grad_tail)
     s.tiles_t[...] = s.tiles[...].T
     s.hidden_t[...] = silu_act(s.hid_pre[...]).T
     s.hid_pre[...] = silu_slope(s.hid_pre[...])
@@ -636,12 +633,13 @@
     greeted = greet()
     t = split_tables(s.tables)
 
-    s.wait("img")
+    for name in ("img", "embed", "first", "second", "head"):
+        s.wait(name)
     cut_tiles(s.img, s.tiles)
     alpha = encode(s)
     s.wait("screens")
+    s.wait("tables")
     pupil_field(alpha, s.screens, s.spread, s.field)
-    s.wait("tables")
     pupil_rows(s, t)
     mine = lax.rem(lax.axis_index("frame"), 2)
     burst = SpectralExchange(s, spectral_sems)
@@ -659,11 +657,9 @@
     burst.finish()
     losses.append((1 - mine, focal_adjoint(s, t, 1 - mine)))
     d_alpha = alpha_adjoint(s, t)
-    alpha_ref[:, 0:modes] = d_alpha.T
 
     early = GradientGroup(((s.grad_tail, 0), (s.grad_first, 128)), buffers[:6], early_sems)
     late = GradientGroup(((s.grad_embed, 0),), buffers[6:], late_sems)
-    s.grad_tail[...] = jnp.zeros_like(s.grad_tail)
     d_pooled = gradients_after_mean(s, d_alpha)
     lane = lax.broadcasted_iota(jnp.int32, (1, side), 1)
     row = jnp.zeros((1, side), jnp.float32)
@@ -677,16 +673,17 @@
     late.send_core(0)
     early.send_plane()
     late.send_plane()
+    alpha_ref[:, 0:modes] = d_alpha.T
     early.send_column()
     late.send_column()
     early.send_back()
     late.send_back()
     early.pass_on()
+    late.pass_on()
     early.finish((s.tail, total_ref.at[256:512]))
     total_ref[512:768, :] = gradient_second(s, s.tail)
     total_ref[768 : 768 + modes, :] = s.tail[0:modes, :]
     loss_ref[...] = s.tail[loss_row : loss_row + 1, 0:side] * (1.0 / frames_total)
-    late.pass_on()
     late.finish((total_ref.at[0:256],))
 
 

time: 60.6 us -> 57.4 us (0.947)
  Pallas kernels: 59.7 us -> 56.7 us
    pallas_call x1, Pallas kernels: 58.8 us -> 55.7 us  [local(): pl.pallas_call(functools.partial(kernel, names, frames_total), out_shape=...]
where the time goes in v6:
time: 57.4 us; the launch traced here: 57.3 us
  Pallas kernels  56.7 us (99%)
  between operations  0.64 us (1%)
    pallas_call x1, Pallas kernels, local(): pl.pallas_call(functools.partial(kernel, names, frames_total), out_shape=...  55.7 us

profile of v6, /device:TPU:1, one launch (start us, length us, event | category | flops | bytes accessed | tf_op | source)
XLA Modules:
  0.0 57.3 jit_solution(2902384558609688114)
XLA Ops:
  0.6 55.7 %shard_map.118 = (f32[8,128]{1,0:T(8,128)S(1)}, f32[1,128]{1,0:T(1,128)S(1)}, f32[816,256]{1,0:T(8,128)S(1)}) custom-call(f32[8,128,128]{2,1,0:T(8,128)} %bitcast.4, f32[256,256]{1,0:T(8,128)} %refs_1_.1, f32[256,256]{1,0:T(8,128)} %refs_2_.1, f32[256,256]{1,0:T(8,128)} %refs_3_.1, f32[44,256]{1,0:T(8,128)} %bitcast.5, f32[1680,256]{1,0:T(8,128)} %constant.2.clone.refs_5_, ...), custom_call_target="tpu_custom_call" | custom-call | tf_op jit(solution)/shard_map/pallas_call | solution.py:725
  56.4 0.9 %shard_map.119 = (f32[256,256]{1,0:T(8,128)}, f32[256,256]{1,0:T(8,128)}, f32[256,256]{1,0:T(8,128)}, f32[44,256]{1,0:T(8,128)}, f32[2,4,44]{2,1,0:T(4,128)}, /*index=5*/f32[1,2]{1,0:T(1,128)}) custom-call(f32[8,128]{1,0:T(8,128)S(1)} %get-tuple-element.15.alpha_ref, f32[1,128]{1,0:T(1,128)S(1)} %get-tuple-element.16.loss_ref, ...), custom_call_target="tpu_custom_call" | custom-call | tf_op jit(solution)/shard_map/pallas_call | solution.py:749

commit v7 on v6

--- a/solution.py
+++ b/solution.py
@@ -136,9 +136,10 @@
     s.inn_pre[...] = pre
     total = tile_sum(silu_act(pre))
     s.inner_sum[...] = total
-    mean = (tile_sum(hidden) + dot(total, s.second[...], HIGHEST)) * (1.0 / tiles_each)
-    s.pooled[...] = mean
-    return dot_nt(mean, s.head[...], HIGHEST)
+    hidden_sum = tile_sum(hidden)
+    s.hidden_sum[...] = hidden_sum
+    alpha = dot_nt(hidden_sum, s.head[...], HIGHEST) + dot_nt(total, s.second_head[...], HIGHEST)
+    return alpha * (1.0 / tiles_each)
 
 
 def chop(value, bits):
@@ -179,7 +180,7 @@
     width = 13
 
     def rows(block, carry):
-        at = [pl.multiple_of((block * width + i) * side, side) for i in range(width)]
+        at = [(block * width + i) * side for i in range(width)]
         total = [jnp.zeros((images, side), jnp.float32) for _ in range(width)]
         for m in range(modes):
             weight = spread[m]
@@ -189,12 +190,13 @@
             up = block * width + i - half // 2
             inside = lane * lane + up * up <= (side // 4) ** 2
             cos, sin = cos_sin(total[i])
-            at = pl.ds(pl.multiple_of((block * width + i) * images, images), images)
+            at = pl.ds((block * width + i) * images, images)
             field[at, 0:side] = jnp.where(inside, cos, 0.0)
             field[at, side : 2 * side] = jnp.where(inside, sin, 0.0)
         return carry
 
-    lax.fori_loop(0, span // width, rows, 0)
+    for block in range(span // width):
+        rows(block, 0)
     field[span * images :, :] = jnp.zeros(((pad_span - span) * images, 2 * side), jnp.float32)
 
 
@@ -243,6 +245,8 @@
     for n in range(images):
         at = n % frames_here
         s.energy[n // frames_here, at : at + 1, :] = jnp.sum(s.img[n] * s.img[n], axis=0, keepdims=True)
+    pooled = s.hidden_sum[...] + dot(s.inner_sum[...], s.second[...])
+    s.pooled[...] = pooled * (1.0 / tiles_each)
     s.grad_tail[...] = jnp.zeros_like(s.grad_tail)
     s.tiles_t[...] = s.tiles[...].T
     s.hidden_t[...] = silu_act(s.hid_pre[...]).T
@@ -341,7 +345,8 @@
 def gradients_after_mean(s, d_alpha):
     s.grad_tail[0:modes, :] = dot(d_alpha, s.pooled[...])
     s.grad_tail[second_row : second_row + modes, :] = dot(d_alpha, s.inner_sum[...])
-    return dot_tn(d_alpha, s.head[...]) * (1.0 / tiles_each)
+    d_pooled = dot_tn(d_alpha, s.head[...]) * (1.0 / tiles_each)
+    return d_pooled, dot_tn(d_alpha, s.second_head[...]) * (1.0 / tiles_each)
 
 
 def gradient_second(s, tail):
@@ -349,8 +354,8 @@
     return dot_tn(factor, s.head[...], HIGHEST) * (1.0 / tiles_each)
 
 
-def gradient_first(s, d_pooled):
-    d_inner = spread(dot_nt(d_pooled, s.second[...])) * s.inn_pre[...]
+def gradient_first(s, d_inner):
+    d_inner = spread(d_inner) * s.inn_pre[...]
     s.grad_first[...] = dot(s.hidden_t[...], d_inner)
     return d_inner
 
@@ -368,6 +373,8 @@
     hidden_t=(256, images * tiles_each),
     inner_sum=(images, 256),
     pooled=(images, 256),
+    hidden_sum=(images, 256),
+    second_head=(modes, 256),
     energy=(images // frames_here, frames_here, side),
     spread=(modes, images, side),
     field=(pad_span * images, 2 * side),
@@ -635,6 +642,7 @@
 
     for name in ("img", "embed", "first", "second", "head"):
         s.wait(name)
+    s.second_head[...] = dot_nt(s.head[...], s.second[...], HIGHEST)
     cut_tiles(s.img, s.tiles)
     alpha = encode(s)
     s.wait("screens")
@@ -660,14 +668,14 @@
 
     early = GradientGroup(((s.grad_tail, 0), (s.grad_first, 128)), buffers[:6], early_sems)
     late = GradientGroup(((s.grad_embed, 0),), buffers[6:], late_sems)
-    d_pooled = gradients_after_mean(s, d_alpha)
+    d_pooled, d_inner = gradients_after_mean(s, d_alpha)
     lane = lax.broadcasted_iota(jnp.int32, (1, side), 1)
     row = jnp.zeros((1, side), jnp.float32)
     for p, loss in losses:
         row = jnp.where(lane == lax.axis_index("dp") * len(losses) + p, loss, row)
     s.grad_tail[loss_row : loss_row + 1, 0:side] = row
     early.send_core(0)
-    d_inner = gradient_first(s, d_pooled)
+    d_inner = gradient_first(s, d_inner)
     early.send_core(1)
     gradient_embed(s, d_pooled, d_inner)
     late.send_core(0)

time: 57.4 us -> 57 us (level)
  no operation moved by 1% of the time
where the time goes in v7:
time: 57 us
  Pallas kernels  56.3 us (99%)
  between operations  0.64 us (1%)
    pallas_call x1, Pallas kernels, local(): pl.pallas_call(functools.partial(kernel, names, frames_total), out_shape=...  55.4 us

profile of v7, /device:TPU:1, one launch (start us, length us, event | category | flops | bytes accessed | tf_op | source)
XLA Modules:
  0.0 57.0 jit_solution(7703189398036847004)
XLA Ops:
  0.6 55.4 %shard_map.118 = (f32[8,128]{1,0:T(8,128)S(1)}, f32[1,128]{1,0:T(1,128)S(1)}, f32[816,256]{1,0:T(8,128)S(1)}) custom-call(f32[8,128,128]{2,1,0:T(8,128)} %bitcast.4, f32[256,256]{1,0:T(8,128)} %refs_1_.1, f32[256,256]{1,0:T(8,128)} %refs_2_.1, f32[256,256]{1,0:T(8,128)} %refs_3_.1, f32[44,256]{1,0:T(8,128)} %bitcast.5, f32[1680,256]{1,0:T(8,128)} %constant.2.clone.refs_5_, ...), custom_call_target="tpu_custom_call" | custom-call | tf_op jit(solution)/shard_map/pallas_call | solution.py:733
  56.0 0.9 %shard_map.119 = (f32[256,256]{1,0:T(8,128)}, f32[256,256]{1,0:T(8,128)}, f32[256,256]{1,0:T(8,128)}, f32[44,256]{1,0:T(8,128)}, f32[2,4,44]{2,1,0:T(4,128)}, /*index=5*/f32[1,2]{1,0:T(1,128)}) custom-call(f32[8,128]{1,0:T(8,128)S(1)} %get-tuple-element.15.alpha_ref, f32[1,128]{1,0:T(1,128)S(1)} %get-tuple-element.16.loss_ref, ...), custom_call_target="tpu_custom_call" | custom-call | tf_op jit(solution)/shard_map/pallas_call | solution.py:757
